TPU v7x, 32 devices: a whole 2x2x4 slice. The times are simulated.
32 devices in a mesh: tm: 16 (over z, x, core), head: 2 (over y).
Axes of the slice: x: 2, y: 2, z: 4, core: 2. Of those that a mesh axis runs over, the one named last changes fastest.
Arguments:
- query_states: bfloat16 [24576, 1024], P('tm', 'head'), may hold values from -30 to 30
- key_states: bfloat16 [24576, 1024], P('tm', 'head'), may hold values from -30 to 30
- value_states: bfloat16 [24576, 1024], P('tm', 'head'), may hold values from -6 to 6
- win_start: int32 [32], P('tm'), may hold values from 0 to 30, as said below
- group_end: int32 [32], P('tm'), may hold values from 0 to 31, as said below
- out_weight: bfloat16 [1024, 1536], replicated, may hold values from -0.1875 to 0.1875
Outputs:
- projected: bfloat16 [24576, 1536], P(('tm', 'head'))
Inputs may be any that keep to these rules, and one draw needn't show every extreme that they name: For every frame f, win_start[f] = max(f - lag, 0) with a lag of 1 to 3; frame 32 - 2 has a lag of 3 in every draw, and the last frame has a lag of 1. `group_end`: frames 2p and 2p + 1 form one group (both end at 2p + 1) or two groups of one frame (each ends at itself); both kinds occur in every draw.
All inputs are finite; a program needn't handle non-finite values.
Results may differ from a plain program's by a relative error of at most 0.0051.
Values may be sent and summed in bfloat16 or wider, within the bound.
No kernel may reach another device: no remote copies, remote signals or barrier semaphores. Data moves between devices by JAX's collectives and lax.ppermute only.
A program may use at most 384 MiB of HBM per device.

v0:
```python
import functools

import jax
import jax.numpy as jnp
from jax import lax
from jax.experimental import pallas as pl
from jax.experimental.pallas import tpu as pltpu
from jax.sharding import PartitionSpec as P

HD = 128
FT = 768
BK = 256
LOG2E = 1.4426950408889634
SCALE = HD ** -0.5 * LOG2E
LIMIT = 1e30
HIDDEN = 1e30
PARAMS = pltpu.CompilerParams(vmem_limit_bytes=12 * 1024 * 1024)
ANY_SPEC = pl.BlockSpec(memory_space=pl.ANY)
NEAR_COST = pl.CostEstimate(flops=8_000_000_000, bytes_accessed=1000, transcendentals=0)
COST = pl.CostEstimate(flops=1000, bytes_accessed=1000, transcendentals=0)
TOKEN = jax.ShapeDtypeStruct((8, 128), jnp.float32)


def dot(a, b):
    return jnp.dot(a, b, preferred_element_type=jnp.float32)


def span(start, size):
    return pl.ds(pl.multiple_of(start, size), size)


def rows_of(slot):
    return slice(slot * FT, (slot + 1) * FT)


def add_frame(lanes, kt, values, block):
    units = [(n, row) for n in range(len(lanes)) for row in range(0, FT, block)]

    def scores(unit):
        n, row = unit
        return dot(lanes[n][0][row : row + block, :], kt[...])

    ahead = scores(units[0])
    for at, (n, row) in enumerate(units):
        s = ahead
        if at + 1 < len(units):
            ahead = scores(units[at + 1])
        _, shift, add = lanes[n]
        weights = [
            jnp.exp2(s[:, c : c + HD] * SCALE - shift[row : row + block, :]).astype(jnp.bfloat16)
            for c in range(0, FT, HD)
        ]
        add(row, dot(jnp.concatenate(weights, axis=1), values[...]))


def visible(info, slot, frame):
    return (frame >= 1) & (frame >= info[2 + slot]) & (frame <= info[4 + slot])


def lanes_of(h, heads):
    share = HD // heads
    lane = lax.broadcasted_iota(jnp.int32, (1, HD), 1)
    return (lane >= h * share) & (lane < (h + 1) * share)


def spread(packed, h, heads):
    row = lax.broadcasted_iota(jnp.int32, (HD, HD), 0)
    chosen = jnp.where(row == h * (HD // heads), 1.0, 0.0).astype(jnp.bfloat16)
    high = packed.astype(jnp.bfloat16)
    low = (packed - high.astype(jnp.float32)).astype(jnp.bfloat16)
    return dot(high, chosen) + dot(low, chosen)


def shift_of(own, seen):
    return jnp.where(seen, own.astype(jnp.float32) * SCALE, HIDDEN)


def sums_into(acc_from, acc, sums, slot, column, h, heads):
    def add(row, added):
        rows = slice(slot * FT + row, slot * FT + row + added.shape[0])
        new = added[:, :HD]
        acc[rows, column] = new if acc_from is None else acc_from[rows, column] + new
        old = sums[rows, :]
        sums[rows, :] = jnp.where(lanes_of(h, heads), old + added[:, HD:], old)

    return add


def load_frame(kt, values, k, v, column):
    kt[...] = k[:, column].T
    values[:, :HD] = v[:, column]


def each_head(group, turn, part=None):
    offset, heads = group
    first, count = part or (0, heads)

    def body(h, carry):
        turn(h, span(h * HD, HD), span((h + offset) * HD, HD))
        return carry

    lax.fori_loop(first, first + count, body, 0)


def own_kernel(group, info, q, k, v, *refs):
    own, acc, sums, token, kt, values = refs
    heads = group[1]
    first = info[0]
    token[...] = jnp.zeros_like(token)
    values[:, HD:] = jnp.ones((FT, HD), jnp.bfloat16)
    ones = jnp.ones((HD, HD), jnp.bfloat16)
    sums[...] = jnp.zeros_like(sums)

    def turn(h, column, wide):
        for slot in (0, 1):
            rows = rows_of(slot)
            product = q[rows, wide].astype(jnp.float32) * k[rows, wide].astype(jnp.float32)
            own[rows, column] = dot(product.astype(jnp.bfloat16), ones).astype(jnp.bfloat16)
        for frame in (0, 1):
            load_frame(kt, values, k.at[rows_of(frame)], v.at[rows_of(frame)], wide)
            lanes = []
            for slot in (0, 1):
                rows = rows_of(slot)
                shift = shift_of(own[rows, column], visible(info, slot, first + frame))
                add = sums_into(acc if frame else None, acc, sums, slot, column, h, heads)
                lanes.append((q[rows, wide], shift, add))
            add_frame(lanes, kt, values, 256)

    each_head(group, turn)


def near_kernel(group, info, q, own, acc_in, sums_in, near_k, near_v, *refs):
    acc, sums, token, kt, values, k_buf, v_buf, sem = refs
    offset, heads = group
    token[...] = jnp.zeros_like(token)
    first = info[0]
    order = (1, 0)
    copies = {
        frame: [
            pltpu.make_async_copy(
                source.at[pl.ds(frame * FT, FT), pl.ds(offset * HD, heads * HD)],
                buf.at[frame],
                sem.at[frame, n],
            )
            for n, (source, buf) in enumerate(((near_k, k_buf), (near_v, v_buf)))
        ]
        for frame in order
    }
    for frame in order:
        for copy in copies[frame]:
            copy.start()
    values[:, HD:] = jnp.ones((FT, HD), jnp.bfloat16)
    sums[...] = sums_in[...]
    for frame in order:
        for copy in copies[frame]:
            copy.wait()

        def turn(h, column, wide):
            load_frame(kt, values, k_buf.at[frame], v_buf.at[frame], column)
            acc_from = acc_in if frame == order[0] else acc
            lanes = []
            for slot in (0, 1):
                rows = rows_of(slot)
                add = sums_into(acc_from, acc, sums, slot, column, h, heads)
                shift = shift_of(own[rows, column], visible(info, slot, first - 2 + frame))
                lanes.append((q[rows, wide], shift, add))
            add_frame(lanes, kt, values, 256)

        each_head(group, turn)


def final_kernel(
    group, part, info, q, own, acc_in, sums_in,
    sink_a, sink_b, far, relay, key_any, value_any, near_k, near_v, *refs,
):
    outs = refs[:-9]
    kt, values, k_buf, v_buf, results, acc, shift, too_large, sem = refs[-9:]
    first = info[0]
    core = info[6]
    far_seen = visible(info, 0, first - 3)
    offset, heads = group
    group_columns = pl.ds(offset * HD, heads * HD)
    part_first, part_heads = part
    values[:, HD:] = jnp.ones((FT, HD), jnp.bfloat16)

    own_columns = pl.ds(0, heads * HD)

    def copies(frame, k, k_row, v, v_row, columns):
        return [
            pltpu.make_async_copy(
                source.at[pl.ds(row, FT), columns], buf.at[frame], sem.at[frame, n]
            )
            for n, (source, row, buf) in enumerate(((k, k_row, k_buf), (v, v_row, v_buf)))
        ]

    arriving = {
        0: [
            (0, sink_a, 0, sink_b, 0, own_columns),
            (1, far, 0, far, FT, own_columns),
        ],
        1: [
            (0, sink_b, 0, sink_a, 0, own_columns),
            (1, relay, 0, relay, FT, group_columns),
        ],
    }
    for which, listed in arriving.items():

        @pl.when(core == which)
        def _():
            started = [copies(*entry) for entry in listed]
            for act in (lambda copy: copy.start(), lambda copy: copy.wait()):
                for pair in started:
                    for copy in pair:
                        act(copy)

    def write(slot, h, acc, total):
        attended = (acc / total).astype(jnp.bfloat16)
        column = span((h - part_first) * HD, HD)
        if len(outs) == 1:
            outs[0][span(slot * FT, FT), column] = attended
        else:

            @pl.when(info[1] == slot)
            def _():
                outs[0][:, column] = attended

            @pl.when(info[1] != slot)
            def _():
                outs[1][:, column] = attended

    def turn(h, column, wide):
        def into(ref, slot, old=None):
            def add(row, added):
                rows = slice(slot * FT + row, slot * FT + row + added.shape[0])
                ref[rows, :] = added if old is None else old[rows, :] + added

            return add

        def lane(slot, seen, add):
            rows = rows_of(slot)
            return q[rows, wide], shift_of(own[rows, column], seen), add

        load_frame(kt, values, k_buf.at[0], v_buf.at[0], column)
        add_frame([lane(slot, True, into(results, slot)) for slot in (1, 0)], kt, values, 256)
        load_frame(kt, values, k_buf.at[1], v_buf.at[1], column)
        add_frame([lane(0, far_seen, into(results, 0, results))], kt, values, 256)
        for slot in (0, 1):
            rows = rows_of(slot)
            total = spread(sums_in[rows, :], h, heads) + results[rows, HD:]
            write(slot, h, acc_in[rows, column] + results[rows, :HD], total)
            too_large[h, slot] = jnp.max(jnp.where(total < LIMIT, 0.0, 1.0))

    each_head(group, turn, part)

    def again(slot, h, column, wide):
        here, there = core == 0, core == 1
        far_here = far_seen & (slot == 0)
        sources = [
            (here, sink_a, 0, sink_b, 0, column), (there, sink_b, 0, sink_a, 0, column),
            (far_here & here, far, 0, far, FT, column),
            (far_here & there, relay, 0, relay, FT, wide),
        ]
        for frame in (0, 1):
            row = frame * FT
            shown = visible(info, slot, first + frame)
            sources.append((shown, key_any, row, value_any, row, wide))
            behind = visible(info, slot, first - 2 + frame)
            sources.append((behind, near_k, row, near_v, row, wide))
        one = (k_buf.at[0, :, :HD], v_buf.at[0, :, :HD])

        def sweep(step):
            def visit(t, carry):
                seen = False
                for n, (shown, k, k_row, v, v_row, where) in enumerate(sources):
                    chosen = (t == n) & shown
                    seen = seen | chosen

                    @pl.when(chosen)
                    def _():
                        for n, (ref, row) in enumerate(((k, k_row), (v, v_row))):
                            copy = pltpu.make_async_copy(
                                ref.at[pl.ds(row, FT), where], one[n], sem.at[0, n]
                            )
                            copy.start()
                            copy.wait()

                @pl.when(seen)
                def _():
                    load_frame(kt, values, k_buf.at[0], v_buf.at[0], slice(0, HD))
                    step()

                return carry

            lax.fori_loop(0, len(sources), visit, 0)

        def by_rows(step):
            def turn(i, carry):
                rows = span(i * HD, HD)
                queries = q[span(slot * FT + i * HD, HD), wide]
                for j in range(0, FT, BK):
                    step(rows, dot(queries, kt[:, j : j + BK]) * SCALE, values[j : j + BK, :])
                return carry

            lax.fori_loop(0, FT // HD, turn, 0)

        def peak(rows, s, _):
            shift[rows, :] = jnp.maximum(shift[rows, :], jnp.max(s, axis=1, keepdims=True))

        def more_sums(rows, s, some_values):
            weights = jnp.concatenate(
                [jnp.exp2(s[:, c : c + HD] - shift[rows, :]) for c in range(0, BK, HD)], axis=1
            )
            acc[rows, :] = acc[rows, :] + dot(weights.astype(jnp.bfloat16), some_values)

        shift[...] = jnp.full((FT, HD), -jnp.inf, jnp.float32)
        acc[...] = jnp.zeros((FT, 2 * HD), jnp.float32)
        sweep(lambda: by_rows(peak))
        sweep(lambda: by_rows(more_sums))
        write(slot, h, acc[:, :HD], acc[:, HD:])

    def check(h, column, wide):
        def turn(slot, carry):
            pl.when(too_large[h, slot] > 0.0)(lambda: again(slot, h, column, wide))
            return carry

        lax.fori_loop(0, 2, turn, 0)

    each_head(group, check, part)


VMEM_SPEC = pl.BlockSpec(memory_space=pltpu.VMEM)
SMEM_SPEC = pl.BlockSpec(memory_space=pltpu.SMEM)


def stage(kernel, arrays, in_any, outs, scratch, cost=None, tokens=()):
    n = len(arrays)

    def run(*refs):
        kernel(*refs[:n], *refs[n + len(tokens) :])

    return pl.pallas_call(
        run,
        in_specs=[SMEM_SPEC] + [VMEM_SPEC] * (n - in_any - 1)
        + [ANY_SPEC] * (in_any + len(tokens)),
        out_specs=[VMEM_SPEC] * len(outs),
        scratch_shapes=[
            pltpu.VMEM((HD, FT), jnp.bfloat16), pltpu.VMEM((FT, 2 * HD), jnp.bfloat16)
        ] + list(scratch),
        out_shape=outs,
        compiler_params=PARAMS,
        cost_estimate=cost or COST,
    )(*arrays, *tokens)


def pick(flag, taken, kept, tokens=(), columns=None):
    column, width = columns or (0, kept.shape[1])

    def kernel(flag, taken, kept, *refs):
        out, sem = refs[-2:]
        for value, source in ((1, taken), (0, kept)):

            @pl.when(flag[0] == value)
            def _():
                rows = source.at[pl.ds(0, FT), pl.ds(column, width)]
                copy = pltpu.make_async_copy(rows, out, sem)
                copy.start()
                copy.wait()

    return pl.pallas_call(
        kernel,
        in_specs=[SMEM_SPEC] + [ANY_SPEC] * (2 + len(tokens)),
        out_specs=VMEM_SPEC,
        out_shape=jax.ShapeDtypeStruct((FT, width), jnp.bfloat16),
        scratch_shapes=[pltpu.SemaphoreType.DMA],
        compiler_params=PARAMS,
        cost_estimate=COST,
    )(jnp.reshape(flag, (1,)).astype(jnp.int32), taken, kept, *tokens)


def last_frames(group, keys, values, tokens=()):
    columns = pl.ds(group[0] * HD, group[1] * HD)
    n = len(tokens)

    def kernel(keys, values, *refs):
        out, sem = refs[n:]
        started = [
            pltpu.make_async_copy(
                source.at[pl.ds(FT, FT), columns], out.at[pl.ds(i * FT, FT)], sem.at[i]
            )
            for i, source in enumerate((keys, values))
        ]
        for copy in started:
            copy.start()
        for copy in started:
            copy.wait()

    return pl.pallas_call(
        kernel,
        in_specs=[ANY_SPEC] * (2 + n),
        out_specs=VMEM_SPEC,
        out_shape=jax.ShapeDtypeStruct((2 * FT, group[1] * HD), jnp.bfloat16),
        scratch_shapes=[pltpu.SemaphoreType.DMA((2,))],
        compiler_params=PARAMS,
        cost_estimate=COST,
    )(keys, values, *tokens)


def sink_steps(size):
    bits = [1 << b for b in range(1, size.bit_length() - 1)]
    orders = (bits[::-1], bits[::-1])
    done = [0, 0]
    steps = []
    for step in range(len(bits)):
        pairs = []
        for which in (0, 1):
            bit = orders[which][step]
            holders = [i for i in range(0, size, 2) if i & ~done[which] == 0]
            pairs += [(i + which, (i | bit) + which) for i in holders]
            done[which] |= bit
        steps.append(pairs)
    return steps


def project(info, parts, weight, base=None, dtype=jnp.bfloat16):
    columns = weight.shape[1]
    turns = 6
    block = columns // turns
    rows = parts[0][0].shape[0]
    n = len(parts)
    bases = [] if base is None else [base]

    def kernel(info, *refs):
        weight, out = refs[n], refs[-1]
        column = span(pl.program_id(0) * block, block)
        total = None if base is None else refs[n + 1][:, column]
        for a, (array, place, received) in zip(refs[:n], parts):
            owner = 1 - info[1] if received else info[1]
            first = owner * (weight.shape[0] // 2) + place
            product = dot(a[...], weight[pl.ds(pl.multiple_of(first, HD), array.shape[1]), column])
            total = product if total is None else total + product
        out[...] = total.astype(dtype)

    return pl.pallas_call(
        kernel,
        grid=(turns,),
        in_specs=[SMEM_SPEC] + [VMEM_SPEC] * (n + 1 + len(bases)),
        out_specs=pl.BlockSpec((rows, block), lambda i: (0, i)),
        out_shape=jax.ShapeDtypeStruct((rows, columns), dtype),
        compiler_params=PARAMS,
        cost_estimate=COST,
    )(info, *[a for a, _, _ in parts], weight, *bases)


def local(query_states, key_states, value_states, win_start, group_end, out_weight):
    axis = "tm"
    size = lax.axis_size(axis)
    paired = lax.axis_size("head") == 2
    me = lax.axis_index(axis)
    core = me % 2
    heads = query_states.shape[1] // HD
    info = jnp.concatenate(
        [
            jnp.stack([me * 2, lax.axis_index("head")]).astype(jnp.int32),
            win_start.astype(jnp.int32),
            group_end.astype(jnp.int32),
            jnp.stack([core]).astype(jnp.int32),
        ]
    )
    groups = [(0, heads // 2), (heads // 2, heads // 2)] if heads % 2 == 0 else [(0, heads)]
    rows = query_states.shape[0]
    group_width = groups[0][1] * HD
    own_like = jax.ShapeDtypeStruct((rows, group_width), jnp.bfloat16)
    acc_like = jax.ShapeDtypeStruct((rows, group_width), jnp.float32)
    sums_like = jax.ShapeDtypeStruct((rows, HD), jnp.float32)
    frame_buffers = [pltpu.VMEM((2, FT, group_width), jnp.bfloat16)] * 2
    dma_sems = pltpu.SemaphoreType.DMA((2, 2))

    onward = [(i, i + 1) for i in range(size - 1)]
    near_k = lax.ppermute(key_states, axis, onward)
    near_v = lax.ppermute(value_states, axis, onward)
    moved = lax.ppermute(value_states, axis, [(0, 1)])
    held = pick(core, moved, key_states)

    def near_stage(group, state, tokens):
        return stage(
            functools.partial(near_kernel, group),
            [info, query_states, *state, near_k, near_v], 2, [acc_like, sums_like, TOKEN],
            frame_buffers + [dma_sems], NEAR_COST, tokens,
        )

    def flag_of(pairs):
        takes = jnp.zeros((), bool)
        for _, target in pairs:
            takes = takes | (me == target)
        return takes

    states = []
    *steps, last_step = sink_steps(size)
    for step, pairs in enumerate(steps):
        moved = lax.ppermute(held, axis, pairs)
        tokens = []
        if step < len(groups):
            *state, token = stage(
                functools.partial(own_kernel, groups[step]),
                [info, query_states, key_states, value_states], 0,
                [own_like, acc_like, sums_like, TOKEN], [], tokens=[held] * (step > 0),
            )
            states.append(state)
            tokens.append(token)
        if step < len(steps) - 1:
            held = pick(flag_of(pairs), moved, held, tokens)

    on_chip = [(i, i + 1) for i in range(0, size, 2)]
    near_last = last_frames((0, heads), near_k, near_v, tokens)
    relay = lax.ppermute(near_last, axis, on_chip)
    own_done, arrivals = tokens, [near_last]
    sends = []
    for g, group in enumerate(groups):
        columns = group[0] * HD, group[1] * HD
        own_last = last_frames(group, key_states, value_states, own_done)
        far = lax.ppermute(own_last, axis, [(i, i + 2) for i in range(0, size - 2, 2)])
        part = pick(flag_of(steps[-1]), moved, held, own_done + arrivals, columns)
        arriving = lax.ppermute(part, axis, last_step)
        if g == 0:
            tokens = []
            for n, state in enumerate(states):
                *sums_now, token = near_stage(groups[n], state, [part])
                states[n] = state[0], *sums_now
                tokens.append(token)
        part = pick(flag_of(last_step), arriving, part, [far] + tokens)
        other = lax.ppermute(part, axis, [(i, i ^ 1) for i in range(size)])
        own_done, arrivals = [part], []
        last = g == len(groups) - 1
        for first, count in [(h, 1) for h in range(group[1])] if last else [(0, group[1])]:
            out = jax.ShapeDtypeStruct((FT if paired else rows, count * HD), jnp.bfloat16)
            results = stage(
                functools.partial(final_kernel, group, (first, count)),
                [info, query_states, *states[g], part, other, far, relay,
                 key_states, value_states, near_k, near_v], 8,
                [out] * (2 if paired else 1),
                frame_buffers + [
                    pltpu.VMEM((rows, 2 * HD), jnp.float32),
                    pltpu.VMEM((FT, 2 * HD), jnp.float32),
                    pltpu.VMEM((FT, HD), jnp.float32),
                    pltpu.SMEM((group[1], 2), jnp.float32),
                    dma_sems,
                ],
            )
            received = None
            if paired:
                received = lax.ppermute(results[1], "head", [(0, 1), (1, 0)])
            sends.append((columns[0] + first * HD, results[0], received))
        tokens = [sends[0][1]]
    if not paired:
        attended = jnp.concatenate([mine for _, mine, _ in sends], axis=1)
        token_rows = lax.all_to_all(attended, "head", split_axis=0, concat_axis=1, tiled=True)
        return dot(token_rows, out_weight).astype(jnp.bfloat16)
    early = [(mine, place, False) for place, mine, _ in sends]
    early.append((sends[0][2], sends[0][0], True))
    late = [(received, place, True) for place, _, received in sends[1:]]
    base = project(info, early, out_weight, dtype=jnp.float32)
    return project(info, late, out_weight, base)


def solution(mesh):
    in_specs = (P("tm", "head"), P("tm", "head"), P("tm", "head"), P("tm"), P("tm"), P())
    out_specs = P(("tm", "head"), None)
    return jax.shard_map(local, mesh=mesh, in_specs=in_specs, out_specs=out_specs, check_vma=False)
```

profile of v0, /device:TPU:18, one launch (start us, length us, event | category | flops | bytes accessed | tf_op | source)
XLA Modules:
  0.0 116.4 jit_solution(5955418043268955653)
XLA Ops:
  0.8 1.9 %collective-permute-start.2 = (bf16[1536,512]{1,0:T(8,128)(2,1)}, bf16[1536,512]{1,0:T(8,128)(2,1)}, u32[]{:S(2)}, u32[]{:S(2)}) collective-permute-start(bf16[1536,512]{1,0:T(8,128)(2,1)} %refs_9_.5), channel_id=1, source_target_pairs={{0,2},{2,4},{4,6},{6,8},{8,10},{10,12},{12,14},{14,16},{16,18},{18... | collective-permute-start | bytes 4718600 | tf_op jit(solution)/shard_map/ppermute | solution.py:479
  7.7 1.7 %collective-permute-start.1 = (bf16[768,512]{1,0:T(8,128)(2,1)}, bf16[768,512]{1,0:T(8,128)(2,1)}, u32[]{:S(2)}, u32[]{:S(2)}) collective-permute-start(bf16[768,512]{1,0:T(8,128)(2,1)} %shard_map.64.kept), channel_id=1, source_target_pairs={{0,16},{2,18},{1,17},{3,19}} | collective-permute-start | bytes 2359304 | tf_op jit(solution)/shard_map/ppermute | solution.py:500
  9.3 3.5 %collective-permute-start.3 = (bf16[1536,512]{1,0:T(8,128)(2,1)S(1)}, bf16[1536,512]{1,0:T(8,128)(2,1)}, u32[]{:S(2)}, u32[]{:S(2)}) collective-permute-start(bf16[1536,512]{1,0:T(8,128)(2,1)S(1)} %copy-done.2), channel_id=1, source_target_pairs={{0,2},{2,4},{4,6},{6,8},{8,10},{10,12},{12,14},{14,16},{16,18},{18... | collective-permute-start | bytes 4718600 | tf_op jit(solution)/shard_map/ppermute | solution.py:480
  13.0 1.4 %copy-done.3 = bf16[1536,512]{1,0:T(8,128)(2,1)S(1)} copy-done((bf16[1536,512]{1,0:T(8,128)(2,1)S(1)}, bf16[1536,512]{1,0:T(8,128)(2,1)}, u32[]{:S(2)}) %copy-start.3) | copy-done | bytes 1572888
  14.4 6.5 %shard_map.65 = (bf16[1536,256]{1,0:T(8,128)(2,1)S(1)}, f32[1536,256]{1,0:T(8,128)S(1)}, f32[1536,128]{1,0:T(8,128)S(1)}, f32[8,128]{1,0:T(8,128)S(1)}) custom-call(s32[7]{0:T(128)S(1)} %concatenate.3.refs_0_.info, bf16[1536,512]{1,0:T(8,128)(2,1)S(1)} %copy-done.3, bf16[1536,512]{1,0:T(8,128)(2,1)S(1)} %copy-done.1, bf16[1536,512]{1,0:T(8,128)(2,1)S(1)} %copy-done.2), custom_call_target="tpu_custom_call" | custom-call | flops 1000 | bytes 1000 | tf_op jit(solution)/shard_map/pallas_call | solution.py:341
  23.9 2.0 %shard_map.66.refs_4_.kept = bf16[768,512]{1,0:T(8,128)(2,1)} custom-call(s32[1]{0:T(128)} %bitcast.3.flag, bf16[768,512]{1,0:T(8,128)(2,1)} %collective-permute-done.1.taken, bf16[768,512]{1,0:T(8,128)(2,1)} %shard_map.64.kept, f32[8,128]{1,0:T(8,128)S(1)} %get-tuple-element.25.refs_0_), custom_call_target="tpu_custom_call" | custom-call | flops 1000 | bytes 1000 | tf_op jit(solution)/shard_map/pallas_call | solution.py:369
  25.9 1.6 %collective-permute-start.4 = (bf16[768,512]{1,0:T(8,128)(2,1)}, bf16[768,512]{1,0:T(8,128)(2,1)}, u32[]{:S(2)}, u32[]{:S(2)}) collective-permute-start(bf16[768,512]{1,0:T(8,128)(2,1)} %shard_map.66.refs_4_.kept), channel_id=1, source_target_pairs={{0,8},{16,24},{2,10},{18,26},{1,9},{17,25},{3,11},{19,27}} | collective-permute-start | bytes 2359304 | tf_op jit(solution)/shard_map/ppermute | solution.py:500
  28.9 6.7 %shard_map.67 = (bf16[1536,256]{1,0:T(8,128)(2,1)S(1)}, f32[1536,256]{1,0:T(8,128)S(1)}, f32[1536,128]{1,0:T(8,128)S(1)}, f32[8,128]{1,0:T(8,128)S(1)}) custom-call(s32[7]{0:T(128)S(1)} %concatenate.3.refs_0_.info, bf16[1536,512]{1,0:T(8,128)(2,1)S(1)} %copy-done.4, bf16[1536,512]{1,0:T(8,128)(2,1)S(1)} %copy-done.1, bf16[1536,512]{1,0:T(8,128)(2,1)S(1)} %copy-done.2, ...), custom_call_target="tpu_custom_call" | custom-call | flops 1000 | bytes 1000 | tf_op jit(solution)/shard_map/pallas_call | solution.py:341
  35.6 3.2 %collective-permute-start.6 = (bf16[1536,256]{1,0:T(8,128)(2,1)S(1)}, bf16[1536,256]{1,0:T(8,128)(2,1)S(1)}, u32[]{:S(2)}, u32[]{:S(2)}) collective-permute-start(bf16[1536,256]{1,0:T(8,128)(2,1)S(1)} %shard_map.71), channel_id=1, source_target_pairs={{0,4},{4,8},{8,12},{12,16},{16,20},{20,24},{24,28},{1,5},{5,9},{9,... | collective-permute-start | bytes 2359304 | tf_op jit(solution)/shard_map/ppermute | solution.py:521
  39.7 1.5 %shard_map.68.refs_1_ = bf16[1536,512]{1,0:T(8,128)(2,1)S(1)} custom-call(bf16[1536,512]{1,0:T(8,128)(2,1)} %collective-permute-done.2.keys.refs_5_.refs_11_, bf16[1536,512]{1,0:T(8,128)(2,1)} %collective-permute-done.3.values.refs_6_.refs_12_, f32[8,128]{1,0:T(8,128)S(1)} %get-tuple-element.29.refs_0_), custom_call_target="tpu_custom_call" | custom-call | flops 1000 | bytes 1000 | tf_op jit(solution)/shard_map/pallas_call | solution.py:397
  43.8 1.5 %collective-permute-start.5 = (bf16[768,256]{1,0:T(8,128)(2,1)S(1)}, bf16[768,256]{1,0:T(8,128)(2,1)S(1)}, u32[]{:S(2)}, u32[]{:S(2)}) collective-permute-start(bf16[768,256]{1,0:T(8,128)(2,1)S(1)} %shard_map.69.refs_7_.kept), channel_id=1, source_target_pairs={{0,4},{8,12},{16,20},{24,28},{2,6},{10,14},{18,22},{26,30},{1,5},{... | collective-permute-start | bytes 1179656 | tf_op jit(solution)/shard_map/ppermute | solution.py:523
  45.3 7.9 %shard_map.72 = (f32[1536,256]{1,0:T(8,128)S(1)}, f32[1536,128]{1,0:T(8,128)S(1)}, f32[8,128]{1,0:T(8,128)S(1)}) custom-call(s32[7]{0:T(128)S(1)} %concatenate.3.refs_0_.info, bf16[1536,512]{1,0:T(8,128)(2,1)S(1)} %copy-done.5, bf16[1536,256]{1,0:T(8,128)(2,1)S(1)} %copy-done.10, f32[1536,256]{1,0:T(8,128)S(1)} %copy-done.12, f32[1536,128]{1,0:T(8,128)S(1)} %copy-done.14, ...), custom_call_target="tpu_custom_call" | custom-call | flops 8000000000 | bytes 1000 | tf_op jit(solution)/shard_map/pallas_call | solution.py:341
  53.2 7.8 %shard_map.70 = (f32[1536,256]{1,0:T(8,128)S(1)}, f32[1536,128]{1,0:T(8,128)S(1)}, f32[8,128]{1,0:T(8,128)S(1)}) custom-call(s32[7]{0:T(128)S(1)} %concatenate.3.refs_0_.info, bf16[1536,512]{1,0:T(8,128)(2,1)S(1)} %copy-done.5, bf16[1536,256]{1,0:T(8,128)(2,1)S(1)} %get-tuple-element.26.refs_2_, f32[1536,256]{1,0:T(8,128)S(1)} %get-tuple-element.27.refs_3_, ...), custom_call_target="tpu_custom_call" | custom-call | flops 8000000000 | bytes 1000 | tf_op jit(solution)/shard_map/pallas_call | solution.py:341
  61.0 3.7 %collective-permute-done.5.taken = bf16[768,256]{1,0:T(8,128)(2,1)S(1)} collective-permute-done((bf16[768,256]{1,0:T(8,128)(2,1)S(1)}, bf16[768,256]{1,0:T(8,128)(2,1)S(1)}, u32[]{:S(2)}, u32[]{:S(2)}) %collective-permute-start.5) | collective-permute-done | bytes 393248 | tf_op jit(solution)/shard_map/ppermute | solution.py:523
  65.0 10.4 %collective-permute-start.8 = (bf16[1536,256]{1,0:T(8,128)(2,1)S(1)}, bf16[1536,256]{1,0:T(8,128)(2,1)S(1)}, u32[]{:S(2)}, u32[]{:S(2)}) collective-permute-start(bf16[1536,256]{1,0:T(8,128)(2,1)S(1)} %shard_map.75), channel_id=1, source_target_pairs={{0,4},{4,8},{8,12},{12,16},{16,20},{20,24},{24,28},{1,5},{5,9},{9,... | collective-permute-start | bytes 2359304 | tf_op jit(solution)/shard_map/ppermute | solution.py:521
  77.8 7.5 %shard_map.76 = (bf16[768,256]{1,0:T(8,128)(2,1)S(1)}, bf16[768,256]{1,0:T(8,128)(2,1)S(1)}) custom-call(s32[7]{0:T(128)S(1)} %concatenate.3.refs_0_.info, bf16[1536,512]{1,0:T(8,128)(2,1)S(1)} %copy-done.5, bf16[1536,256]{1,0:T(8,128)(2,1)S(1)} %copy-done.10, f32[1536,256]{1,0:T(8,128)S(1)} %get-tuple-element.37.refs_3_, ...), custom_call_target="tpu_custom_call" | custom-call | flops 1000 | bytes 1000 | tf_op jit(solution)/shard_map/pallas_call | solution.py:341
  85.3 6.5 %collective-permute-done.7.taken = bf16[768,256]{1,0:T(8,128)(2,1)S(1)} collective-permute-done((bf16[768,256]{1,0:T(8,128)(2,1)S(1)}, bf16[768,256]{1,0:T(8,128)(2,1)S(1)}, u32[]{:S(2)}, u32[]{:S(2)}) %collective-permute-start.7) | collective-permute-done | bytes 393248 | tf_op jit(solution)/shard_map/ppermute | solution.py:523
  92.1 1.6 %collective-permute-start.14 = (bf16[768,256]{1,0:T(8,128)(2,1)S(1)}, bf16[768,256]{1,0:T(8,128)(2,1)S(1)}, u32[]{:S(2)}, u32[]{:S(2)}) collective-permute-start(bf16[768,256]{1,0:T(8,128)(2,1)S(1)} %get-tuple-element.44), channel_id=1, source_target_pairs={{0,1},{1,0},{2,3},{3,2},{4,5},{5,4},{6,7},{7,6},{8,9},{9,8},{10,11... | collective-permute-start | bytes 1179656 | tf_op jit(solution)/shard_map/ppermute | solution.py:551
  93.9 4.6 %shard_map.79 = (bf16[768,128]{1,0:T(8,128)(2,1)S(1)}, bf16[768,128]{1,0:T(8,128)(2,1)S(1)}) custom-call(s32[7]{0:T(128)S(1)} %concatenate.3.refs_0_.info, bf16[1536,512]{1,0:T(8,128)(2,1)S(1)} %copy-done.5, bf16[1536,256]{1,0:T(8,128)(2,1)S(1)} %get-tuple-element.26.refs_2_, f32[1536,256]{1,0:T(8,128)S(1)} %get-tuple-element.30.refs_3_, ...), custom_call_target="tpu_custom_call" | custom-call | flops 1000 | bytes 1000 | tf_op jit(solution)/shard_map/pallas_call | solution.py:341
  98.4 1.6 %collective-permute-start.13 = (bf16[768,128]{1,0:T(8,128)(2,1)S(1)}, bf16[768,128]{1,0:T(8,128)(2,1)S(1)}, u32[]{:S(2)}, u32[]{:S(2)}) collective-permute-start(bf16[768,128]{1,0:T(8,128)(2,1)S(1)} %get-tuple-element.41), channel_id=1, source_target_pairs={{0,1},{1,0},{2,3},{3,2},{4,5},{5,4},{6,7},{7,6},{8,9},{9,8},{10,11... | collective-permute-start | bytes 589832 | tf_op jit(solution)/shard_map/ppermute | solution.py:551
  100.0 4.3 %shard_map.78 = (bf16[768,128]{1,0:T(8,128)(2,1)S(1)}, bf16[768,128]{1,0:T(8,128)(2,1)S(1)}) custom-call(s32[7]{0:T(128)S(1)} %concatenate.3.refs_0_.info, bf16[1536,512]{1,0:T(8,128)(2,1)S(1)} %copy-done.5, bf16[1536,256]{1,0:T(8,128)(2,1)S(1)} %get-tuple-element.26.refs_2_, f32[1536,256]{1,0:T(8,128)S(1)} %get-tuple-element.30.refs_3_, ...), custom_call_target="tpu_custom_call" | custom-call | flops 1000 | bytes 1000 | tf_op jit(solution)/shard_map/pallas_call | solution.py:341
  105.0 4.3 %shard_map.80.refs_3_ = f32[768,1536]{1,0:T(8,128)S(1)} custom-call(s32[7]{0:T(128)S(1)} %concatenate.3.refs_0_.info, bf16[768,256]{1,0:T(8,128)(2,1)S(1)} %get-tuple-element.39.refs_1_.refs_0_, bf16[768,128]{1,0:T(8,128)(2,1)S(1)} %get-tuple-element.42.refs_1_, bf16[768,128]{1,0:T(8,128)(2,1)S(1)} %get-tuple-element.43.refs_2_, ...), custom_call_target="tpu_custom_call" | custom-call | flops 1000 | bytes 1000 | tf_op jit(solution)/shard_map/pallas_call | solution.py:443
  109.3 2.8 %collective-permute-done.12.refs_0_ = bf16[768,128]{1,0:T(8,128)(2,1)S(1)} collective-permute-done((bf16[768,128]{1,0:T(8,128)(2,1)S(1)}, bf16[768,128]{1,0:T(8,128)(2,1)S(1)}, u32[]{:S(2)}, u32[]{:S(2)}) %collective-permute-start.12) | collective-permute-done | bytes 196640 | tf_op jit(solution)/shard_map/ppermute | solution.py:551
  112.1 4.2 %shard_map.81 = bf16[768,1536]{1,0:T(8,128)(2,1)} custom-call(s32[7]{0:T(128)S(1)} %concatenate.3.refs_0_.info, bf16[768,128]{1,0:T(8,128)(2,1)S(1)} %collective-permute-done.12.refs_0_, bf16[768,128]{1,0:T(8,128)(2,1)S(1)} %collective-permute-done.13.refs_1_, bf16[1024,1536]{1,0:T(8,128)(2,1)S(1)} %copy-done.6, f32[768,1536]{1,0:T(8,128)S(1)} %shard_map.80.refs_3_), custom_call_target="tpu_custom_call" | custom-call | flops 1000 | bytes 1000 | tf_op jit(solution)/shard_map/pallas_call | solution.py:443
  (59 shorter events, 17.3 us)
Async XLA Ops:
  0.0 2.7 %collective-permute-start = (bf16[1536,512]{1,0:T(8,128)(2,1)}, bf16[1536,512]{1,0:T(8,128)(2,1)S(1)}, u32[]{:S(2)}, u32[]{:S(2)}) collective-permute-start(bf16[1536,512]{1,0:T(8,128)(2,1)} %refs_10_.5), channel_id=1, source_target_pairs={{0,2},{1,3}} | collective-permute-start | bytes 4718600 | tf_op jit(solution)/shard_map/ppermute | solution.py:481
  0.8 38.1 %collective-permute-start.2 = (bf16[1536,512]{1,0:T(8,128)(2,1)}, bf16[1536,512]{1,0:T(8,128)(2,1)}, u32[]{:S(2)}, u32[]{:S(2)}) collective-permute-start(bf16[1536,512]{1,0:T(8,128)(2,1)} %refs_9_.5), channel_id=1, source_target_pairs={{0,2},{2,4},{4,6},{6,8},{8,10},{10,12},{12,14},{14,16},{16,18},{18... | collective-permute-start | bytes 4718600 | tf_op jit(solution)/shard_map/ppermute | solution.py:479
  6.7 2.7 %copy-start.2 = (bf16[1536,512]{1,0:T(8,128)(2,1)S(1)}, bf16[1536,512]{1,0:T(8,128)(2,1)}, u32[]{:S(2)}) copy-start(bf16[1536,512]{1,0:T(8,128)(2,1)} %refs_10_.5) | copy-start | bytes 4718596
  6.7 6.2 %copy-start.15 = (s32[2]{0:T(128)S(1)}, s32[2]{0:T(128)}, u32[]{:S(2)}) copy-start(s32[2]{0:T(128)} %param.9) | copy-start | bytes 28
  6.7 6.2 %copy-start.16 = (s32[2]{0:T(128)S(1)}, s32[2]{0:T(128)}, u32[]{:S(2)}) copy-start(s32[2]{0:T(128)} %param.10) | copy-start | bytes 28
  6.7 6.3 %copy-start.1 = (bf16[1536,512]{1,0:T(8,128)(2,1)S(1)}, bf16[1536,512]{1,0:T(8,128)(2,1)}, u32[]{:S(2)}) copy-start(bf16[1536,512]{1,0:T(8,128)(2,1)} %refs_9_.5) | copy-start | bytes 4718596
  7.7 16.2 %collective-permute-start.1 = (bf16[768,512]{1,0:T(8,128)(2,1)}, bf16[768,512]{1,0:T(8,128)(2,1)}, u32[]{:S(2)}, u32[]{:S(2)}) collective-permute-start(bf16[768,512]{1,0:T(8,128)(2,1)} %shard_map.64.kept), channel_id=1, source_target_pairs={{0,16},{2,18},{1,17},{3,19}} | collective-permute-start | bytes 2359304 | tf_op jit(solution)/shard_map/ppermute | solution.py:500
  9.3 30.3 %collective-permute-start.3 = (bf16[1536,512]{1,0:T(8,128)(2,1)S(1)}, bf16[1536,512]{1,0:T(8,128)(2,1)}, u32[]{:S(2)}, u32[]{:S(2)}) collective-permute-start(bf16[1536,512]{1,0:T(8,128)(2,1)S(1)} %copy-done.2), channel_id=1, source_target_pairs={{0,2},{2,4},{4,6},{6,8},{8,10},{10,12},{12,14},{14,16},{16,18},{18... | collective-permute-start | bytes 4718600 | tf_op jit(solution)/shard_map/ppermute | solution.py:480
  25.9 16.7 %collective-permute-start.4 = (bf16[768,512]{1,0:T(8,128)(2,1)}, bf16[768,512]{1,0:T(8,128)(2,1)}, u32[]{:S(2)}, u32[]{:S(2)}) collective-permute-start(bf16[768,512]{1,0:T(8,128)(2,1)} %shard_map.66.refs_4_.kept), channel_id=1, source_target_pairs={{0,8},{16,24},{2,10},{18,26},{1,9},{17,25},{3,11},{19,27}} | collective-permute-start | bytes 2359304 | tf_op jit(solution)/shard_map/ppermute | solution.py:500
  35.6 25.4 %collective-permute-start.6 = (bf16[1536,256]{1,0:T(8,128)(2,1)S(1)}, bf16[1536,256]{1,0:T(8,128)(2,1)S(1)}, u32[]{:S(2)}, u32[]{:S(2)}) collective-permute-start(bf16[1536,256]{1,0:T(8,128)(2,1)S(1)} %shard_map.71), channel_id=1, source_target_pairs={{0,4},{4,8},{8,12},{12,16},{16,20},{20,24},{24,28},{1,5},{5,9},{9,... | collective-permute-start | bytes 2359304 | tf_op jit(solution)/shard_map/ppermute | solution.py:521
  39.7 5.6 %copy-start.12 = (f32[1536,256]{1,0:T(8,128)S(1)}, f32[1536,256]{1,0:T(8,128)}, u32[]{:S(2)}) copy-start(f32[1536,256]{1,0:T(8,128)} %copy-done.11) | copy-start | bytes 4718596
  41.2 36.6 %collective-permute-start.10 = (bf16[1536,512]{1,0:T(8,128)(2,1)S(1)}, bf16[1536,512]{1,0:T(8,128)(2,1)S(1)}, u32[]{:S(2)}, u32[]{:S(2)}) collective-permute-start(bf16[1536,512]{1,0:T(8,128)(2,1)S(1)} %shard_map.68.refs_1_), channel_id=1, source_target_pairs={{0,2},{4,6},{8,10},{12,14},{16,18},{20,22},{24,26},{28,30},{1,3},{... | collective-permute-start | bytes 4718600 | tf_op jit(solution)/shard_map/ppermute | solution.py:515
  42.6 2.7 %copy-start.5 = (bf16[1536,512]{1,0:T(8,128)(2,1)S(1)}, bf16[1536,512]{1,0:T(8,128)(2,1)}, u32[]{:S(2)}) copy-start(bf16[1536,512]{1,0:T(8,128)(2,1)} %refs_1_.13) | copy-start | bytes 4718596
  42.6 2.7 %copy-start.10 = (bf16[1536,256]{1,0:T(8,128)(2,1)S(1)}, bf16[1536,256]{1,0:T(8,128)(2,1)}, u32[]{:S(2)}) copy-start(bf16[1536,256]{1,0:T(8,128)(2,1)} %copy-done.9) | copy-start | bytes 2359300
  42.6 2.7 %copy-start.14 = (f32[1536,128]{1,0:T(8,128)S(1)}, f32[1536,128]{1,0:T(8,128)}, u32[]{:S(2)}) copy-start(f32[1536,128]{1,0:T(8,128)} %copy-done.13) | copy-start | bytes 2359300
  43.8 20.9 %collective-permute-start.5 = (bf16[768,256]{1,0:T(8,128)(2,1)S(1)}, bf16[768,256]{1,0:T(8,128)(2,1)S(1)}, u32[]{:S(2)}, u32[]{:S(2)}) collective-permute-start(bf16[768,256]{1,0:T(8,128)(2,1)S(1)} %shard_map.69.refs_7_.kept), channel_id=1, source_target_pairs={{0,4},{8,12},{16,20},{24,28},{2,6},{10,14},{18,22},{26,30},{1,5},{... | collective-permute-start | bytes 1179656 | tf_op jit(solution)/shard_map/ppermute | solution.py:523
  65.0 26.9 %collective-permute-start.8 = (bf16[1536,256]{1,0:T(8,128)(2,1)S(1)}, bf16[1536,256]{1,0:T(8,128)(2,1)S(1)}, u32[]{:S(2)}, u32[]{:S(2)}) collective-permute-start(bf16[1536,256]{1,0:T(8,128)(2,1)S(1)} %shard_map.75), channel_id=1, source_target_pairs={{0,4},{4,8},{8,12},{12,16},{16,20},{20,24},{24,28},{1,5},{5,9},{9,... | collective-permute-start | bytes 2359304 | tf_op jit(solution)/shard_map/ppermute | solution.py:521
  75.4 2.4 %collective-permute-start.9 = (bf16[768,256]{1,0:T(8,128)(2,1)S(1)}, bf16[768,256]{1,0:T(8,128)(2,1)S(1)}, u32[]{:S(2)}, u32[]{:S(2)}) collective-permute-start(bf16[768,256]{1,0:T(8,128)(2,1)S(1)} %shard_map.73.refs_0_.refs_5_), channel_id=1, source_target_pairs={{0,2},{2,0},{4,6},{6,4},{8,10},{10,8},{12,14},{14,12},{16,18},{18,... | collective-permute-start | bytes 1179656 | tf_op jit(solution)/shard_map/ppermute | solution.py:531
  76.5 15.4 %collective-permute-start.7 = (bf16[768,256]{1,0:T(8,128)(2,1)S(1)}, bf16[768,256]{1,0:T(8,128)(2,1)S(1)}, u32[]{:S(2)}, u32[]{:S(2)}) collective-permute-start(bf16[768,256]{1,0:T(8,128)(2,1)S(1)} %shard_map.74.kept), channel_id=1, source_target_pairs={{0,4},{8,12},{16,20},{24,28},{2,6},{10,14},{18,22},{26,30},{1,5},{... | collective-permute-start | bytes 1179656 | tf_op jit(solution)/shard_map/ppermute | solution.py:523
  92.1 1.8 %collective-permute-start.11 = (bf16[768,256]{1,0:T(8,128)(2,1)S(1)}, bf16[768,256]{1,0:T(8,128)(2,1)S(1)}, u32[]{:S(2)}, u32[]{:S(2)}) collective-permute-start(bf16[768,256]{1,0:T(8,128)(2,1)S(1)} %shard_map.77.refs_5_), channel_id=1, source_target_pairs={{0,2},{2,0},{4,6},{6,4},{8,10},{10,8},{12,14},{14,12},{16,18},{18,... | collective-permute-start | bytes 1179656 | tf_op jit(solution)/shard_map/ppermute | solution.py:531
  92.1 12.8 %collective-permute-start.14 = (bf16[768,256]{1,0:T(8,128)(2,1)S(1)}, bf16[768,256]{1,0:T(8,128)(2,1)S(1)}, u32[]{:S(2)}, u32[]{:S(2)}) collective-permute-start(bf16[768,256]{1,0:T(8,128)(2,1)S(1)} %get-tuple-element.44), channel_id=1, source_target_pairs={{0,1},{1,0},{2,3},{3,2},{4,5},{5,4},{6,7},{7,6},{8,9},{9,8},{10,11... | collective-permute-start | bytes 1179656 | tf_op jit(solution)/shard_map/ppermute | solution.py:551
  98.4 10.8 %collective-permute-start.13 = (bf16[768,128]{1,0:T(8,128)(2,1)S(1)}, bf16[768,128]{1,0:T(8,128)(2,1)S(1)}, u32[]{:S(2)}, u32[]{:S(2)}) collective-permute-start(bf16[768,128]{1,0:T(8,128)(2,1)S(1)} %get-tuple-element.41), channel_id=1, source_target_pairs={{0,1},{1,0},{2,3},{3,2},{4,5},{5,4},{6,7},{7,6},{8,9},{9,8},{10,11... | collective-permute-start | bytes 589832 | tf_op jit(solution)/shard_map/ppermute | solution.py:551
  100.0 4.9 %copy-start.6 = (bf16[1024,1536]{1,0:T(8,128)(2,1)S(1)}, bf16[1024,1536]{1,0:T(8,128)(2,1)}, u32[]{:S(2)}) copy-start(bf16[1024,1536]{1,0:T(8,128)(2,1)} %refs_2_.5) | copy-start | bytes 9437188
  104.4 7.7 %collective-permute-start.12 = (bf16[768,128]{1,0:T(8,128)(2,1)S(1)}, bf16[768,128]{1,0:T(8,128)(2,1)S(1)}, u32[]{:S(2)}, u32[]{:S(2)}) collective-permute-start(bf16[768,128]{1,0:T(8,128)(2,1)S(1)} %get-tuple-element.40), channel_id=1, source_target_pairs={{0,1},{1,0},{2,3},{3,2},{4,5},{5,4},{6,7},{7,6},{8,9},{9,8},{10,11... | collective-permute-start | bytes 589832 | tf_op jit(solution)/shard_map/ppermute | solution.py:551
  (8 other events, 9.7 us)
where the time goes:
time: 118 us; the launch traced here: 116 us
  Pallas kernels  61 us (52%)
  starting transfers between devices  31.1 us (26%)
  waiting for transfers between devices  14 us (12%)
  local copies, waits for them, and re-layouts  9.83 us (8%)
    pallas_call x7, Pallas kernels, stage(): pl.pallas_call(run, in_specs=[SMEM_SPEC] + [VMEM_SPEC] * (n - in_any - 1)...  45.2 us
    ppermute x2, starting transfers between devices, local(): lax.ppermute(own_last, axis, [(i, i + 2) for i in range(0, size - 2, 2)])  13.6 us
    ppermute x2, waiting for transfers between devices, local(): arriving = lax.ppermute(part, axis, last_step)  10.2 us
    unnamed x34, local copies, waits for them, and re-layouts  9.76 us
    pallas_call x2, Pallas kernels, project(): pl.pallas_call(kernel, grid=(turns,), in_specs=[SMEM_SPEC] + [VMEM_SPEC]...  8.55 us
    pallas_call x6, Pallas kernels, pick(): pl.pallas_call(kernel, in_specs=[SMEM_SPEC] + [ANY_SPEC] * (2 + len(token...  5.57 us
    ppermute x3, starting transfers between devices, local(): received = lax.ppermute(results[1], 'head', [(0, 1), (1, 0)])  3.74 us
    ppermute x1, starting transfers between devices, local(): near_v = lax.ppermute(value_states, axis, onward)  3.55 us
  transfers between devices with their start and end apart: 15, of which 5 were waited for; matrix products, arithmetic and copies ran while one was open for 0% of the time, Pallas kernels for 49%

commit v1 on v0

--- a/solution.py
+++ b/solution.py
@@ -479,7 +479,7 @@
     near_k = lax.ppermute(key_states, axis, onward)
     near_v = lax.ppermute(value_states, axis, onward)
     moved = lax.ppermute(value_states, axis, [(0, 1)])
-    held = pick(core, moved, key_states)
+    held = jnp.where(core == 0, key_states[:FT], moved[:FT])
 
     def near_stage(group, state, tokens):
         return stage(
@@ -513,23 +513,24 @@
     on_chip = [(i, i + 1) for i in range(0, size, 2)]
     near_last = last_frames((0, heads), near_k, near_v, tokens)
     relay = lax.ppermute(near_last, axis, on_chip)
-    own_done, arrivals = tokens, [near_last]
+    before, arrivals = tokens, [near_last]
+    halves = []
+    near_after = []
+    for g, group in enumerate(groups):
+        columns = group[0] * HD, group[1] * HD
+        own_last = last_frames(group, key_states, value_states, before)
+        far = lax.ppermute(own_last, axis, [(i, i + 2) for i in range(0, size - 2, 2)])
+        part = pick(flag_of(steps[-1]), moved, held, before + arrivals, columns)
+        before, arrivals = [part], []
+        arriving = lax.ppermute(part, axis, last_step)
+        *sums_now, token = near_stage(group, states[g], near_after + [part])
+        states[g] = states[g][0], *sums_now
+        part = pick(flag_of(last_step), arriving, part, [far, token])
+        near_after = [part]
+        halves.append((part, lax.ppermute(part, axis, [(i, i ^ 1) for i in range(size)]), far))
     sends = []
     for g, group in enumerate(groups):
-        columns = group[0] * HD, group[1] * HD
-        own_last = last_frames(group, key_states, value_states, own_done)
-        far = lax.ppermute(own_last, axis, [(i, i + 2) for i in range(0, size - 2, 2)])
-        part = pick(flag_of(steps[-1]), moved, held, own_done + arrivals, columns)
-        arriving = lax.ppermute(part, axis, last_step)
-        if g == 0:
-            tokens = []
-            for n, state in enumerate(states):
-                *sums_now, token = near_stage(groups[n], state, [part])
-                states[n] = state[0], *sums_now
-                tokens.append(token)
-        part = pick(flag_of(last_step), arriving, part, [far] + tokens)
-        other = lax.ppermute(part, axis, [(i, i ^ 1) for i in range(size)])
-        own_done, arrivals = [part], []
+        part, other, far = halves[g]
         last = g == len(groups) - 1
         for first, count in [(h, 1) for h in range(group[1])] if last else [(0, group[1])]:
             out = jax.ShapeDtypeStruct((FT if paired else rows, count * HD), jnp.bfloat16)
@@ -549,8 +550,7 @@
             received = None
             if paired:
                 received = lax.ppermute(results[1], "head", [(0, 1), (1, 0)])
-            sends.append((columns[0] + first * HD, results[0], received))
-        tokens = [sends[0][1]]
+            sends.append(((group[0] + first) * HD, results[0], received))
     if not paired:
         attended = jnp.concatenate([mine for _, mine, _ in sends], axis=1)
         token_rows = lax.all_to_all(attended, "head", split_axis=0, concat_axis=1, tiled=True)

time: 118 us -> 112 us (0.949); the launches traced: 116 us -> 112 us
  waiting for transfers between devices: 14 us -> 6.28 us
  other arithmetic: 0 us -> 2.1 us
    ppermute x2, waiting for transfers between devices: 10.2 us -> 0.01 us  [local(): arriving = lax.ppermute(part, axis, last_step)]
    ppermute x2, waiting for transfers between devices: 0.01 us -> 3.96 us  [local(): lax.ppermute(own_last, axis, [(i, i + 2) for i in range(0, size - 2, 2)])]
    select_n x0 -> x1, other arithmetic: none -> 2.1 us  [local(): held = jnp.where(core == 0, key_states[:FT], moved[:FT])]
    unnamed x34 -> x42, local copies, waits for them, and re-layouts: 9.76 us -> 8.91 us
    pallas_call x6 -> x5, Pallas kernels: 5.57 us -> 4.92 us  [pick(): pl.pallas_call(kernel, in_specs=[SMEM_SPEC] + [ANY_SPEC] * (2 + len(token...]
  transfers between devices with their start and end apart: 15 -> 15, of which waited for: 5 -> 3; matrix products, arithmetic and copies ran while one was open for 0% -> 2% of each run, Pallas kernels for 49% -> 52%
where the time goes in v1:
time: 112 us
  Pallas kernels  62 us (55%)
  starting transfers between devices  31.8 us (28%)
  local copies, waits for them, and re-layouts  8.98 us (8%)
  waiting for transfers between devices  6.28 us (6%)
  other arithmetic  2.1 us (2%)
    pallas_call x7, Pallas kernels, stage(): pl.pallas_call(run, in_specs=[SMEM_SPEC] + [VMEM_SPEC] * (n - in_any - 1)...  46 us
    ppermute x2, starting transfers between devices, local(): lax.ppermute(own_last, axis, [(i, i + 2) for i in range(0, size - 2, 2)])  14.3 us
    unnamed x42, local copies, waits for them, and re-layouts  8.91 us
    pallas_call x2, Pallas kernels, project(): pl.pallas_call(kernel, grid=(turns,), in_specs=[SMEM_SPEC] + [VMEM_SPEC]...  8.55 us
    pallas_call x5, Pallas kernels, pick(): pl.pallas_call(kernel, in_specs=[SMEM_SPEC] + [ANY_SPEC] * (2 + len(token...  4.92 us
    ppermute x2, waiting for transfers between devices, local(): lax.ppermute(own_last, axis, [(i, i + 2) for i in range(0, size - 2, 2)])  3.96 us
    ppermute x3, starting transfers between devices, local(): received = lax.ppermute(results[1], 'head', [(0, 1), (1, 0)])  3.74 us
    ppermute x1, starting transfers between devices, local(): near_v = lax.ppermute(value_states, axis, onward)  3.57 us
  transfers between devices with their start and end apart: 15, of which 3 were waited for; matrix products, arithmetic and copies ran while one was open for 2% of the time, Pallas kernels for 52%

profile of v1, /device:TPU:18, one launch (start us, length us, event | category | flops | bytes accessed | tf_op | source)
XLA Modules:
  0.0 111.7 jit_solution(5511015518847749551)
XLA Ops:
  0.9 1.9 %collective-permute-start.2 = (bf16[1536,512]{1,0:T(8,128)(2,1)}, bf16[1536,512]{1,0:T(8,128)(2,1)}, u32[]{:S(2)}, u32[]{:S(2)}) collective-permute-start(bf16[1536,512]{1,0:T(8,128)(2,1)} %refs_9_.5), channel_id=1, source_target_pairs={{0,2},{2,4},{4,6},{6,8},{8,10},{10,12},{12,14},{14,16},{16,18},{18... | collective-permute-start | bytes 4718600 | tf_op jit(solution)/shard_map/ppermute | solution.py:479
  2.9 2.1 %slice_select_fusion.kept = bf16[768,512]{1,0:T(8,128)(2,1)} fusion(bf16[1536,512]{1,0:T(8,128)(2,1)S(1)} %collective-permute-done, bf16[1536,512]{1,0:T(8,128)(2,1)} %refs_9_.5, pred[]{:T(512)S(6)} %eq.61), kind=kLoop, calls=%fused_computation | loop fusion | flops 393216 | bytes 2359297 | tf_op jit(solution)/shard_map/jit(_where)/select_n | solution.py:482
  5.0 1.5 %collective-permute-start.1 = (bf16[768,512]{1,0:T(8,128)(2,1)}, bf16[768,512]{1,0:T(8,128)(2,1)}, u32[]{:S(2)}, u32[]{:S(2)}) collective-permute-start(bf16[768,512]{1,0:T(8,128)(2,1)} %slice_select_fusion.kept), channel_id=1, source_target_pairs={{0,16},{2,18},{1,17},{3,19}} | collective-permute-start | bytes 2359304 | tf_op jit(solution)/shard_map/ppermute | solution.py:500
  6.5 3.6 %collective-permute-start.3 = (bf16[1536,512]{1,0:T(8,128)(2,1)}, bf16[1536,512]{1,0:T(8,128)(2,1)}, u32[]{:S(2)}, u32[]{:S(2)}) collective-permute-start(bf16[1536,512]{1,0:T(8,128)(2,1)} %refs_10_.5), channel_id=1, source_target_pairs={{0,2},{2,4},{4,6},{6,8},{8,10},{10,12},{12,14},{14,16},{16,18},{18... | collective-permute-start | bytes 4718600 | tf_op jit(solution)/shard_map/ppermute | solution.py:480
  10.2 1.4 %copy-done.1 = bf16[1536,512]{1,0:T(8,128)(2,1)S(1)} copy-done((bf16[1536,512]{1,0:T(8,128)(2,1)S(1)}, bf16[1536,512]{1,0:T(8,128)(2,1)}, u32[]{:S(2)}) %copy-start.1) | copy-done | bytes 1572888
  13.0 6.6 %shard_map.64 = (bf16[1536,256]{1,0:T(8,128)(2,1)S(1)}, f32[1536,256]{1,0:T(8,128)S(1)}, f32[1536,128]{1,0:T(8,128)S(1)}, f32[8,128]{1,0:T(8,128)S(1)}) custom-call(s32[7]{0:T(128)S(1)} %concatenate.3.refs_0_.info, bf16[1536,512]{1,0:T(8,128)(2,1)S(1)} %copy-done.3, bf16[1536,512]{1,0:T(8,128)(2,1)S(1)} %copy-done, bf16[1536,512]{1,0:T(8,128)(2,1)S(1)} %copy-done.1), custom_call_target="tpu_custom_call" | custom-call | flops 1000 | bytes 1000 | tf_op jit(solution)/shard_map/pallas_call | solution.py:341
  22.6 2.2 %shard_map.65.refs_4_.kept = bf16[768,512]{1,0:T(8,128)(2,1)} custom-call(s32[1]{0:T(128)} %bitcast.3.flag, bf16[768,512]{1,0:T(8,128)(2,1)} %collective-permute-done.1.taken, bf16[768,512]{1,0:T(8,128)(2,1)} %slice_select_fusion.kept, f32[8,128]{1,0:T(8,128)S(1)} %get-tuple-element.25.refs_0_), custom_call_target="tpu_custom_call" | custom-call | flops 1000 | bytes 1000 | tf_op jit(solution)/shard_map/pallas_call | solution.py:369
  24.7 1.6 %collective-permute-start.4 = (bf16[768,512]{1,0:T(8,128)(2,1)}, bf16[768,512]{1,0:T(8,128)(2,1)}, u32[]{:S(2)}, u32[]{:S(2)}) collective-permute-start(bf16[768,512]{1,0:T(8,128)(2,1)} %shard_map.65.refs_4_.kept), channel_id=1, source_target_pairs={{0,8},{16,24},{2,10},{18,26},{1,9},{17,25},{3,11},{19,27}} | collective-permute-start | bytes 2359304 | tf_op jit(solution)/shard_map/ppermute | solution.py:500
  26.3 1.4 %copy-done.4 = bf16[1536,512]{1,0:T(8,128)(2,1)S(1)} copy-done((bf16[1536,512]{1,0:T(8,128)(2,1)S(1)}, bf16[1536,512]{1,0:T(8,128)(2,1)}, u32[]{:S(2)}) %copy-start.4) | copy-done | bytes 1572888
  27.7 6.5 %shard_map.66 = (bf16[1536,256]{1,0:T(8,128)(2,1)S(1)}, f32[1536,256]{1,0:T(8,128)S(1)}, f32[1536,128]{1,0:T(8,128)S(1)}, f32[8,128]{1,0:T(8,128)S(1)}) custom-call(s32[7]{0:T(128)S(1)} %concatenate.3.refs_0_.info, bf16[1536,512]{1,0:T(8,128)(2,1)S(1)} %copy-done.4, bf16[1536,512]{1,0:T(8,128)(2,1)S(1)} %copy-done, bf16[1536,512]{1,0:T(8,128)(2,1)S(1)} %copy-done.2, ...), custom_call_target="tpu_custom_call" | custom-call | flops 1000 | bytes 1000 | tf_op jit(solution)/shard_map/pallas_call | solution.py:341
  36.2 3.1 %collective-permute-start.6 = (bf16[1536,256]{1,0:T(8,128)(2,1)}, bf16[1536,256]{1,0:T(8,128)(2,1)}, u32[]{:S(2)}, u32[]{:S(2)}) collective-permute-start(bf16[1536,256]{1,0:T(8,128)(2,1)} %shard_map.69), channel_id=1, source_target_pairs={{0,4},{4,8},{8,12},{12,16},{16,20},{20,24},{24,28},{1,5},{5,9},{9,... | collective-permute-start | bytes 2359304 | tf_op jit(solution)/shard_map/ppermute | solution.py:522
  46.2 1.4 %collective-permute-start.7 = (bf16[768,256]{1,0:T(8,128)(2,1)S(1)}, bf16[768,256]{1,0:T(8,128)(2,1)S(1)}, u32[]{:S(2)}, u32[]{:S(2)}) collective-permute-start(bf16[768,256]{1,0:T(8,128)(2,1)S(1)} %shard_map.72.refs_8_.kept), channel_id=1, source_target_pairs={{0,4},{8,12},{16,20},{24,28},{2,6},{10,14},{18,22},{26,30},{1,5},{... | collective-permute-start | bytes 1179656 | tf_op jit(solution)/shard_map/ppermute | solution.py:525
  47.7 11.2 %collective-permute-start.8 = (bf16[1536,256]{1,0:T(8,128)(2,1)S(1)}, bf16[1536,256]{1,0:T(8,128)(2,1)S(1)}, u32[]{:S(2)}, u32[]{:S(2)}) collective-permute-start(bf16[1536,256]{1,0:T(8,128)(2,1)S(1)} %shard_map.74), channel_id=1, source_target_pairs={{0,4},{4,8},{8,12},{12,16},{16,20},{20,24},{24,28},{1,5},{5,9},{9,... | collective-permute-start | bytes 2359304 | tf_op jit(solution)/shard_map/ppermute | solution.py:522
  58.9 7.9 %shard_map.70 = (f32[1536,256]{1,0:T(8,128)S(1)}, f32[1536,128]{1,0:T(8,128)S(1)}, f32[8,128]{1,0:T(8,128)S(1)}) custom-call(s32[7]{0:T(128)S(1)} %concatenate.3.refs_0_.info, bf16[1536,512]{1,0:T(8,128)(2,1)S(1)} %copy-done.5, bf16[1536,256]{1,0:T(8,128)(2,1)S(1)} %copy-done.10, f32[1536,256]{1,0:T(8,128)S(1)} %copy-done.12, f32[1536,128]{1,0:T(8,128)S(1)} %copy-done.16, ...), custom_call_target="tpu_custom_call" | custom-call | flops 8000000000 | bytes 1000 | tf_op jit(solution)/shard_map/pallas_call | solution.py:341
  68.2 7.8 %shard_map.73 = (f32[1536,256]{1,0:T(8,128)S(1)}, f32[1536,128]{1,0:T(8,128)S(1)}, f32[8,128]{1,0:T(8,128)S(1)}) custom-call(s32[7]{0:T(128)S(1)} %concatenate.3.refs_0_.info, bf16[1536,512]{1,0:T(8,128)(2,1)S(1)} %copy-done.5, bf16[1536,256]{1,0:T(8,128)(2,1)S(1)} %copy-done.8, f32[1536,256]{1,0:T(8,128)S(1)} %copy-done.14, f32[1536,128]{1,0:T(8,128)S(1)} %copy-done.18, ...), custom_call_target="tpu_custom_call" | custom-call | flops 8000000000 | bytes 1000 | tf_op jit(solution)/shard_map/pallas_call | solution.py:341
  76.0 4.0 %collective-permute-done.8.refs_0_.refs_7_ = bf16[1536,256]{1,0:T(8,128)(2,1)S(1)} collective-permute-done((bf16[1536,256]{1,0:T(8,128)(2,1)S(1)}, bf16[1536,256]{1,0:T(8,128)(2,1)S(1)}, u32[]{:S(2)}, u32[]{:S(2)}) %collective-permute-start.8) | collective-permute-done | bytes 786464 | tf_op jit(solution)/shard_map/ppermute | solution.py:522
  80.2 8.2 %shard_map.78 = (bf16[768,256]{1,0:T(8,128)(2,1)S(1)}, bf16[768,256]{1,0:T(8,128)(2,1)S(1)}) custom-call(s32[7]{0:T(128)S(1)} %concatenate.3.refs_0_.info, bf16[1536,512]{1,0:T(8,128)(2,1)S(1)} %copy-done.5, bf16[1536,256]{1,0:T(8,128)(2,1)S(1)} %copy-done.10, f32[1536,256]{1,0:T(8,128)S(1)} %get-tuple-element.39.refs_3_, ...), custom_call_target="tpu_custom_call" | custom-call | flops 1000 | bytes 1000 | tf_op jit(solution)/shard_map/pallas_call | solution.py:341
  88.5 1.6 %collective-permute-start.14 = (bf16[768,256]{1,0:T(8,128)(2,1)S(1)}, bf16[768,256]{1,0:T(8,128)(2,1)S(1)}, u32[]{:S(2)}, u32[]{:S(2)}) collective-permute-start(bf16[768,256]{1,0:T(8,128)(2,1)S(1)} %get-tuple-element.44), channel_id=1, source_target_pairs={{0,1},{1,0},{2,3},{3,2},{4,5},{5,4},{6,7},{7,6},{8,9},{9,8},{10,11... | collective-permute-start | bytes 1179656 | tf_op jit(solution)/shard_map/ppermute | solution.py:552
  90.1 4.6 %shard_map.77 = (bf16[768,128]{1,0:T(8,128)(2,1)S(1)}, bf16[768,128]{1,0:T(8,128)(2,1)S(1)}) custom-call(s32[7]{0:T(128)S(1)} %concatenate.3.refs_0_.info, bf16[1536,512]{1,0:T(8,128)(2,1)S(1)} %copy-done.5, bf16[1536,256]{1,0:T(8,128)(2,1)S(1)} %copy-done.8, f32[1536,256]{1,0:T(8,128)S(1)} %get-tuple-element.34.refs_3_, ...), custom_call_target="tpu_custom_call" | custom-call | flops 1000 | bytes 1000 | tf_op jit(solution)/shard_map/pallas_call | solution.py:341
  95.2 4.3 %shard_map.76 = (bf16[768,128]{1,0:T(8,128)(2,1)S(1)}, bf16[768,128]{1,0:T(8,128)(2,1)S(1)}) custom-call(s32[7]{0:T(128)S(1)} %concatenate.3.refs_0_.info, bf16[1536,512]{1,0:T(8,128)(2,1)S(1)} %copy-done.5, bf16[1536,256]{1,0:T(8,128)(2,1)S(1)} %copy-done.8, f32[1536,256]{1,0:T(8,128)S(1)} %get-tuple-element.34.refs_3_, ...), custom_call_target="tpu_custom_call" | custom-call | flops 1000 | bytes 1000 | tf_op jit(solution)/shard_map/pallas_call | solution.py:341
  99.6 1.6 %collective-permute-start.11 = (bf16[768,128]{1,0:T(8,128)(2,1)S(1)}, bf16[768,128]{1,0:T(8,128)(2,1)S(1)}, u32[]{:S(2)}, u32[]{:S(2)}) collective-permute-start(bf16[768,128]{1,0:T(8,128)(2,1)S(1)} %get-tuple-element.37), channel_id=1, source_target_pairs={{0,1},{1,0},{2,3},{3,2},{4,5},{5,4},{6,7},{7,6},{8,9},{9,8},{10,11... | collective-permute-start | bytes 589832 | tf_op jit(solution)/shard_map/ppermute | solution.py:552
  101.2 4.3 %shard_map.79.refs_3_ = f32[768,1536]{1,0:T(8,128)S(1)} custom-call(s32[7]{0:T(128)S(1)} %concatenate.3.refs_0_.info, bf16[768,256]{1,0:T(8,128)(2,1)S(1)} %get-tuple-element.41.refs_0_, bf16[768,128]{1,0:T(8,128)(2,1)S(1)} %get-tuple-element.42.refs_1_, bf16[768,128]{1,0:T(8,128)(2,1)S(1)} %get-tuple-element.43.refs_2_, ...), custom_call_target="tpu_custom_call" | custom-call | flops 1000 | bytes 1000 | tf_op jit(solution)/shard_map/pallas_call | solution.py:443
  105.5 1.9 %collective-permute-done.11.refs_0_ = bf16[768,128]{1,0:T(8,128)(2,1)S(1)} collective-permute-done((bf16[768,128]{1,0:T(8,128)(2,1)S(1)}, bf16[768,128]{1,0:T(8,128)(2,1)S(1)}, u32[]{:S(2)}, u32[]{:S(2)}) %collective-permute-start.11) | collective-permute-done | bytes 196640 | tf_op jit(solution)/shard_map/ppermute | solution.py:552
  107.4 4.2 %shard_map.80 = bf16[768,1536]{1,0:T(8,128)(2,1)} custom-call(s32[7]{0:T(128)S(1)} %concatenate.3.refs_0_.info, bf16[768,128]{1,0:T(8,128)(2,1)S(1)} %collective-permute-done.11.refs_0_, bf16[768,128]{1,0:T(8,128)(2,1)S(1)} %collective-permute-done.12.refs_1_, bf16[1024,1536]{1,0:T(8,128)(2,1)S(1)} %copy-done.6, f32[768,1536]{1,0:T(8,128)S(1)} %shard_map.79.refs_3_), custom_call_target="tpu_custom_call" | custom-call | flops 1000 | bytes 1000 | tf_op jit(solution)/shard_map/pallas_call | solution.py:443
  (67 shorter events, 16.2 us)
Async XLA Ops:
  0.0 10.2 %copy-start = (bf16[1536,512]{1,0:T(8,128)(2,1)S(1)}, bf16[1536,512]{1,0:T(8,128)(2,1)}, u32[]{:S(2)}) copy-start(bf16[1536,512]{1,0:T(8,128)(2,1)} %refs_9_.5) | copy-start | bytes 4718596
  0.0 10.1 %copy-start.20 = (s32[2]{0:T(128)S(1)}, s32[2]{0:T(128)}, u32[]{:S(2)}) copy-start(s32[2]{0:T(128)} %param.10) | copy-start | bytes 28
  0.0 10.1 %copy-start.19 = (s32[2]{0:T(128)S(1)}, s32[2]{0:T(128)}, u32[]{:S(2)}) copy-start(s32[2]{0:T(128)} %param.9) | copy-start | bytes 28
  0.0 2.8 %collective-permute-start = (bf16[1536,512]{1,0:T(8,128)(2,1)}, bf16[1536,512]{1,0:T(8,128)(2,1)S(1)}, u32[]{:S(2)}, u32[]{:S(2)}) collective-permute-start(bf16[1536,512]{1,0:T(8,128)(2,1)} %refs_10_.5), channel_id=1, source_target_pairs={{0,2},{1,3}} | collective-permute-start | bytes 4718600 | tf_op jit(solution)/shard_map/ppermute | solution.py:481
  0.9 38.5 %collective-permute-start.2 = (bf16[1536,512]{1,0:T(8,128)(2,1)}, bf16[1536,512]{1,0:T(8,128)(2,1)}, u32[]{:S(2)}, u32[]{:S(2)}) collective-permute-start(bf16[1536,512]{1,0:T(8,128)(2,1)} %refs_9_.5), channel_id=1, source_target_pairs={{0,2},{2,4},{4,6},{6,8},{8,10},{10,12},{12,14},{14,16},{16,18},{18... | collective-permute-start | bytes 4718600 | tf_op jit(solution)/shard_map/ppermute | solution.py:479
  5.0 17.6 %collective-permute-start.1 = (bf16[768,512]{1,0:T(8,128)(2,1)}, bf16[768,512]{1,0:T(8,128)(2,1)}, u32[]{:S(2)}, u32[]{:S(2)}) collective-permute-start(bf16[768,512]{1,0:T(8,128)(2,1)} %slice_select_fusion.kept), channel_id=1, source_target_pairs={{0,16},{2,18},{1,17},{3,19}} | collective-permute-start | bytes 2359304 | tf_op jit(solution)/shard_map/ppermute | solution.py:500
  6.5 33.3 %collective-permute-start.3 = (bf16[1536,512]{1,0:T(8,128)(2,1)}, bf16[1536,512]{1,0:T(8,128)(2,1)}, u32[]{:S(2)}, u32[]{:S(2)}) collective-permute-start(bf16[1536,512]{1,0:T(8,128)(2,1)} %refs_10_.5), channel_id=1, source_target_pairs={{0,2},{2,4},{4,6},{6,8},{8,10},{10,12},{12,14},{14,16},{16,18},{18... | collective-permute-start | bytes 4718600 | tf_op jit(solution)/shard_map/ppermute | solution.py:480
  24.7 17.9 %collective-permute-start.4 = (bf16[768,512]{1,0:T(8,128)(2,1)}, bf16[768,512]{1,0:T(8,128)(2,1)}, u32[]{:S(2)}, u32[]{:S(2)}) collective-permute-start(bf16[768,512]{1,0:T(8,128)(2,1)} %shard_map.65.refs_4_.kept), channel_id=1, source_target_pairs={{0,8},{16,24},{2,10},{18,26},{1,9},{17,25},{3,11},{19,27}} | collective-permute-start | bytes 2359304 | tf_op jit(solution)/shard_map/ppermute | solution.py:500
  36.2 30.6 %collective-permute-start.6 = (bf16[1536,256]{1,0:T(8,128)(2,1)}, bf16[1536,256]{1,0:T(8,128)(2,1)}, u32[]{:S(2)}, u32[]{:S(2)}) collective-permute-start(bf16[1536,256]{1,0:T(8,128)(2,1)} %shard_map.69), channel_id=1, source_target_pairs={{0,4},{4,8},{8,12},{12,16},{16,20},{20,24},{24,28},{1,5},{5,9},{9,... | collective-permute-start | bytes 2359304 | tf_op jit(solution)/shard_map/ppermute | solution.py:522
  41.2 39.0 %collective-permute-start.10 = (bf16[1536,512]{1,0:T(8,128)(2,1)S(1)}, bf16[1536,512]{1,0:T(8,128)(2,1)S(1)}, u32[]{:S(2)}, u32[]{:S(2)}) collective-permute-start(bf16[1536,512]{1,0:T(8,128)(2,1)S(1)} %shard_map.67.refs_1_), channel_id=1, source_target_pairs={{0,2},{4,6},{8,10},{12,14},{16,18},{20,22},{24,26},{28,30},{1,3},{... | collective-permute-start | bytes 4718600 | tf_op jit(solution)/shard_map/ppermute | solution.py:515
  43.6 23.2 %collective-permute-start.5 = (bf16[768,256]{1,0:T(8,128)(2,1)S(1)}, bf16[768,256]{1,0:T(8,128)(2,1)S(1)}, u32[]{:S(2)}, u32[]{:S(2)}) collective-permute-start(bf16[768,256]{1,0:T(8,128)(2,1)S(1)} %shard_map.68.refs_7_.kept.refs_0_), channel_id=1, source_target_pairs={{0,4},{8,12},{16,20},{24,28},{2,6},{10,14},{18,22},{26,30},{1,5},{... | collective-permute-start | bytes 1179656 | tf_op jit(solution)/shard_map/ppermute | solution.py:525
  44.9 13.9 %copy-start.12 = (f32[1536,256]{1,0:T(8,128)S(1)}, f32[1536,256]{1,0:T(8,128)}, u32[]{:S(2)}) copy-start(f32[1536,256]{1,0:T(8,128)} %copy-done.11) | copy-start | bytes 4718596
  45.0 13.9 %copy-start.16 = (f32[1536,128]{1,0:T(8,128)S(1)}, f32[1536,128]{1,0:T(8,128)}, u32[]{:S(2)}) copy-start(f32[1536,128]{1,0:T(8,128)} %copy-done.15) | copy-start | bytes 2359300
  45.0 13.9 %copy-start.5 = (bf16[1536,512]{1,0:T(8,128)(2,1)S(1)}, bf16[1536,512]{1,0:T(8,128)(2,1)}, u32[]{:S(2)}) copy-start(bf16[1536,512]{1,0:T(8,128)(2,1)} %refs_1_.13) | copy-start | bytes 4718596
  45.1 13.8 %copy-start.10 = (bf16[1536,256]{1,0:T(8,128)(2,1)S(1)}, bf16[1536,256]{1,0:T(8,128)(2,1)}, u32[]{:S(2)}) copy-start(bf16[1536,256]{1,0:T(8,128)(2,1)} %copy-done.9) | copy-start | bytes 2359300
  46.2 29.7 %collective-permute-start.7 = (bf16[768,256]{1,0:T(8,128)(2,1)S(1)}, bf16[768,256]{1,0:T(8,128)(2,1)S(1)}, u32[]{:S(2)}, u32[]{:S(2)}) collective-permute-start(bf16[768,256]{1,0:T(8,128)(2,1)S(1)} %shard_map.72.refs_8_.kept), channel_id=1, source_target_pairs={{0,4},{8,12},{16,20},{24,28},{2,6},{10,14},{18,22},{26,30},{1,5},{... | collective-permute-start | bytes 1179656 | tf_op jit(solution)/shard_map/ppermute | solution.py:525
  47.7 32.3 %collective-permute-start.8 = (bf16[1536,256]{1,0:T(8,128)(2,1)S(1)}, bf16[1536,256]{1,0:T(8,128)(2,1)S(1)}, u32[]{:S(2)}, u32[]{:S(2)}) collective-permute-start(bf16[1536,256]{1,0:T(8,128)(2,1)S(1)} %shard_map.74), channel_id=1, source_target_pairs={{0,4},{4,8},{8,12},{12,16},{16,20},{20,24},{24,28},{1,5},{5,9},{9,... | collective-permute-start | bytes 2359304 | tf_op jit(solution)/shard_map/ppermute | solution.py:522
  58.9 8.4 %copy-start.14 = (f32[1536,256]{1,0:T(8,128)S(1)}, f32[1536,256]{1,0:T(8,128)}, u32[]{:S(2)}) copy-start(f32[1536,256]{1,0:T(8,128)} %copy-done.13) | copy-start | bytes 4718596
  67.3 13.0 %collective-permute-start.13 = (bf16[768,256]{1,0:T(8,128)(2,1)S(1)}, bf16[768,256]{1,0:T(8,128)(2,1)S(1)}, u32[]{:S(2)}, u32[]{:S(2)}) collective-permute-start(bf16[768,256]{1,0:T(8,128)(2,1)S(1)} %shard_map.71.refs_7_.refs_5_), channel_id=1, source_target_pairs={{0,2},{2,0},{4,6},{6,4},{8,10},{10,8},{12,14},{14,12},{16,18},{18,... | collective-permute-start | bytes 1179656 | tf_op jit(solution)/shard_map/ppermute | solution.py:530
  80.1 9.9 %collective-permute-start.9 = (bf16[768,256]{1,0:T(8,128)(2,1)S(1)}, bf16[768,256]{1,0:T(8,128)(2,1)S(1)}, u32[]{:S(2)}, u32[]{:S(2)}) collective-permute-start(bf16[768,256]{1,0:T(8,128)(2,1)S(1)} %shard_map.75.refs_5_), channel_id=1, source_target_pairs={{0,2},{2,0},{4,6},{6,4},{8,10},{10,8},{12,14},{14,12},{16,18},{18,... | collective-permute-start | bytes 1179656 | tf_op jit(solution)/shard_map/ppermute | solution.py:530
  88.5 12.7 %collective-permute-start.14 = (bf16[768,256]{1,0:T(8,128)(2,1)S(1)}, bf16[768,256]{1,0:T(8,128)(2,1)S(1)}, u32[]{:S(2)}, u32[]{:S(2)}) collective-permute-start(bf16[768,256]{1,0:T(8,128)(2,1)S(1)} %get-tuple-element.44), channel_id=1, source_target_pairs={{0,1},{1,0},{2,3},{3,2},{4,5},{5,4},{6,7},{7,6},{8,9},{9,8},{10,11... | collective-permute-start | bytes 1179656 | tf_op jit(solution)/shard_map/ppermute | solution.py:552
  94.6 10.8 %collective-permute-start.12 = (bf16[768,128]{1,0:T(8,128)(2,1)S(1)}, bf16[768,128]{1,0:T(8,128)(2,1)S(1)}, u32[]{:S(2)}, u32[]{:S(2)}) collective-permute-start(bf16[768,128]{1,0:T(8,128)(2,1)S(1)} %get-tuple-element.38), channel_id=1, source_target_pairs={{0,1},{1,0},{2,3},{3,2},{4,5},{5,4},{6,7},{7,6},{8,9},{9,8},{10,11... | collective-permute-start | bytes 589832 | tf_op jit(solution)/shard_map/ppermute | solution.py:552
  95.2 5.9 %copy-start.6 = (bf16[1024,1536]{1,0:T(8,128)(2,1)S(1)}, bf16[1024,1536]{1,0:T(8,128)(2,1)}, u32[]{:S(2)}) copy-start(bf16[1024,1536]{1,0:T(8,128)(2,1)} %refs_2_.5) | copy-start | bytes 9437188
  99.6 7.8 %collective-permute-start.11 = (bf16[768,128]{1,0:T(8,128)(2,1)S(1)}, bf16[768,128]{1,0:T(8,128)(2,1)S(1)}, u32[]{:S(2)}, u32[]{:S(2)}) collective-permute-start(bf16[768,128]{1,0:T(8,128)(2,1)S(1)} %get-tuple-element.37), channel_id=1, source_target_pairs={{0,1},{1,0},{2,3},{3,2},{4,5},{5,4},{6,7},{7,6},{8,9},{9,8},{10,11... | collective-permute-start | bytes 589832 | tf_op jit(solution)/shard_map/ppermute | solution.py:552
  (12 other events, 18.2 us)

commit v2 on v1

--- a/solution.py
+++ b/solution.py
@@ -195,11 +195,11 @@
 
     arriving = {
         0: [
-            (0, sink_a, 0, sink_b, 0, own_columns),
+            (0, sink_a, 0, sink_b, 0, group_columns),
             (1, far, 0, far, FT, own_columns),
         ],
         1: [
-            (0, sink_b, 0, sink_a, 0, own_columns),
+            (0, sink_b, 0, sink_a, 0, group_columns),
             (1, relay, 0, relay, FT, group_columns),
         ],
     }
@@ -256,7 +256,7 @@
         here, there = core == 0, core == 1
         far_here = far_seen & (slot == 0)
         sources = [
-            (here, sink_a, 0, sink_b, 0, column), (there, sink_b, 0, sink_a, 0, column),
+            (here, sink_a, 0, sink_b, 0, wide), (there, sink_b, 0, sink_a, 0, wide),
             (far_here & here, far, 0, far, FT, column),
             (far_here & there, relay, 0, relay, FT, wide),
         ]
@@ -421,9 +421,8 @@
     return steps
 
 
-def project(info, parts, weight, base=None, dtype=jnp.bfloat16):
+def project(info, parts, weight, base=None, dtype=jnp.bfloat16, turns=6):
     columns = weight.shape[1]
-    turns = 6
     block = columns // turns
     rows = parts[0][0].shape[0]
     n = len(parts)
@@ -511,46 +510,53 @@
             held = pick(flag_of(pairs), moved, held, tokens)
 
     on_chip = [(i, i + 1) for i in range(0, size, 2)]
-    near_last = last_frames((0, heads), near_k, near_v, tokens)
+    own_last = last_frames(groups[0], key_states, value_states, tokens)
+    near_last = last_frames((0, heads), near_k, near_v, [own_last])
     relay = lax.ppermute(near_last, axis, on_chip)
-    before, arrivals = tokens, [near_last]
-    halves = []
-    near_after = []
+    part = pick(flag_of(steps[-1]), moved, held, tokens + [near_last])
+    arriving = lax.ppermute(part, axis, last_step)
+
     for g, group in enumerate(groups):
-        columns = group[0] * HD, group[1] * HD
-        own_last = last_frames(group, key_states, value_states, before)
-        far = lax.ppermute(own_last, axis, [(i, i + 2) for i in range(0, size - 2, 2)])
-        part = pick(flag_of(steps[-1]), moved, held, before + arrivals, columns)
-        before, arrivals = [part], []
-        arriving = lax.ppermute(part, axis, last_step)
-        *sums_now, token = near_stage(group, states[g], near_after + [part])
+        *sums_now, token = near_stage(group, states[g], [part] + tokens)
         states[g] = states[g][0], *sums_now
-        part = pick(flag_of(last_step), arriving, part, [far, token])
-        near_after = [part]
-        halves.append((part, lax.ppermute(part, axis, [(i, i ^ 1) for i in range(size)]), far))
+        tokens = [token]
+
+    def send_far(own_last):
+        return lax.ppermute(own_last, axis, [(i, i + 2) for i in range(0, size - 2, 2)])
+
+    fars = [send_far(own_last)]
+    for group in groups[1:]:
+        own_last = last_frames(group, key_states, value_states, tokens)
+        tokens = tokens + [own_last]
+        fars.append(send_far(own_last))
+    sink = pick(flag_of(last_step), arriving, part, tokens)
+    other = lax.ppermute(sink, axis, [(i, i ^ 1) for i in range(size)])
     sends = []
-    for g, group in enumerate(groups):
-        part, other, far = halves[g]
-        last = g == len(groups) - 1
-        for first, count in [(h, 1) for h in range(group[1])] if last else [(0, group[1])]:
+
+    def finish(g, pieces, far):
+        for first, count in pieces:
             out = jax.ShapeDtypeStruct((FT if paired else rows, count * HD), jnp.bfloat16)
             results = stage(
-                functools.partial(final_kernel, group, (first, count)),
-                [info, query_states, *states[g], part, other, far, relay,
+                functools.partial(final_kernel, groups[g], (first, count)),
+                [info, query_states, *states[g], sink, other, far, relay,
                  key_states, value_states, near_k, near_v], 8,
                 [out] * (2 if paired else 1),
                 frame_buffers + [
                     pltpu.VMEM((rows, 2 * HD), jnp.float32),
                     pltpu.VMEM((FT, 2 * HD), jnp.float32),
                     pltpu.VMEM((FT, HD), jnp.float32),
-                    pltpu.SMEM((group[1], 2), jnp.float32),
+                    pltpu.SMEM((groups[g][1], 2), jnp.float32),
                     dma_sems,
                 ],
             )
             received = None
             if paired:
                 received = lax.ppermute(results[1], "head", [(0, 1), (1, 0)])
-            sends.append(((group[0] + first) * HD, results[0], received))
+            sends.append(((groups[g][0] + first) * HD, results[0], received))
+
+    for g, (_, count) in enumerate(groups):
+        last = g == len(groups) - 1
+        finish(g, [(h, 1) for h in range(count)] if last else [(0, count)], fars[g])
     if not paired:
         attended = jnp.concatenate([mine for _, mine, _ in sends], axis=1)
         token_rows = lax.all_to_all(attended, "head", split_axis=0, concat_axis=1, tiled=True)
@@ -559,7 +565,7 @@
     early.append((sends[0][2], sends[0][0], True))
     late = [(received, place, True) for place, _, received in sends[1:]]
     base = project(info, early, out_weight, dtype=jnp.float32)
-    return project(info, late, out_weight, base)
+    return project(info, late, out_weight, base, turns=3)
 
 
 def solution(mesh):

time: 112 us -> 105 us (0.938)
  starting transfers between devices: 31.8 us -> 22.8 us
  waiting for transfers between devices: 6.28 us -> 13.9 us
  Pallas kernels: 62 us -> 57.1 us
  local copies, waits for them, and re-layouts: 8.98 us -> 7.27 us
    ppermute x2 -> x1, waiting for transfers between devices: 0.01 us -> 9.1 us  [local(): arriving = lax.ppermute(part, axis, last_step)]
    ppermute x7 -> x6, starting transfers between devices: 18.2 us -> 10.3 us  [the longest x2 6.49 us: send_far(): lax.ppermute(own_last, axis, [(i, i + 2) for i in range(0, size - 2, 2)])]
    ppermute x7 -> x6, waiting for transfers between devices: 5.89 us -> 2.6 us  [the longest x2 1.76 us: send_far(): lax.ppermute(own_last, axis, [(i, i + 2) for i in range(0, size - 2, 2)])]
    ppermute x1, waiting for transfers between devices: 0.37 us -> 2.22 us  [local(): near_v = lax.ppermute(value_states, axis, onward)]
    unnamed x42 -> x30, local copies, waits for them, and re-layouts: 8.91 us -> 7.19 us
    pallas_call x7, Pallas kernels: 46 us -> 44.3 us  [stage(): pl.pallas_call(run, in_specs=[SMEM_SPEC] + [VMEM_SPEC] * (n - in_any - 1)...]
    pallas_call x5 -> x3, Pallas kernels: 4.92 us -> 3.51 us  [pick(): pl.pallas_call(kernel, in_specs=[SMEM_SPEC] + [ANY_SPEC] * (2 + len(token...]
    ppermute x2 -> x1, starting transfers between devices: 2.72 us -> 1.6 us  [local(): arriving = lax.ppermute(part, axis, last_step)]
  transfers between devices with their start and end apart: 15 -> 13, of which waited for: 3 -> 4; matrix products, arithmetic and copies ran while one was open for 2% -> 2% of each run, Pallas kernels for 52% -> 52%
where the time goes in v2:
time: 105 us; the launch traced here: 104 us
  Pallas kernels  57.1 us (54%)
  starting transfers between devices  22.8 us (22%)
  waiting for transfers between devices  13.9 us (13%)
  local copies, waits for them, and re-layouts  7.27 us (7%)
  other arithmetic  2.13 us (2%)
    pallas_call x7, Pallas kernels, stage(): pl.pallas_call(run, in_specs=[SMEM_SPEC] + [VMEM_SPEC] * (n - in_any - 1)...  44.3 us
    ppermute x1, waiting for transfers between devices, local(): arriving = lax.ppermute(part, axis, last_step)  9.1 us
    pallas_call x2, Pallas kernels, project(): pl.pallas_call(kernel, grid=(turns,), in_specs=[SMEM_SPEC] + [VMEM_SPEC]...  7.72 us
    unnamed x30, local copies, waits for them, and re-layouts  7.19 us
    ppermute x2, starting transfers between devices, send_far(): lax.ppermute(own_last, axis, [(i, i + 2) for i in range(0, size - 2, 2)])  6.49 us
    ppermute x3, starting transfers between devices, finish(): received = lax.ppermute(results[1], 'head', [(0, 1), (1, 0)])  3.74 us
    ppermute x1, starting transfers between devices, local(): near_v = lax.ppermute(value_states, axis, onward)  3.57 us
    pallas_call x3, Pallas kernels, pick(): pl.pallas_call(kernel, in_specs=[SMEM_SPEC] + [ANY_SPEC] * (2 + len(token...  3.51 us
  transfers between devices with their start and end apart: 13, of which 4 were waited for; matrix products, arithmetic and copies ran while one was open for 2% of the time, Pallas kernels for 52%

profile of v2, /device:TPU:18, one launch (start us, length us, event | category | flops | bytes accessed | tf_op | source)
XLA Modules:
  0.0 103.7 jit_solution(8331425122577197164)
XLA Ops:
  0.9 1.9 %collective-permute-start.2 = (bf16[1536,512]{1,0:T(8,128)(2,1)}, bf16[1536,512]{1,0:T(8,128)(2,1)}, u32[]{:S(2)}, u32[]{:S(2)}) collective-permute-start(bf16[1536,512]{1,0:T(8,128)(2,1)} %refs_9_.5), channel_id=1, source_target_pairs={{0,2},{2,4},{4,6},{6,8},{8,10},{10,12},{12,14},{14,16},{16,18},{18... | collective-permute-start | bytes 4718600 | tf_op jit(solution)/shard_map/ppermute | solution.py:478
  2.9 2.1 %slice_select_fusion.kept = bf16[768,512]{1,0:T(8,128)(2,1)} fusion(bf16[1536,512]{1,0:T(8,128)(2,1)S(1)} %collective-permute-done, bf16[1536,512]{1,0:T(8,128)(2,1)} %refs_9_.5, pred[]{:T(512)S(6)} %eq.49), kind=kLoop, calls=%fused_computation | loop fusion | flops 393216 | bytes 2359297 | tf_op jit(solution)/shard_map/jit(_where)/select_n | solution.py:481
  5.0 1.6 %collective-permute-start.1 = (bf16[768,512]{1,0:T(8,128)(2,1)}, bf16[768,512]{1,0:T(8,128)(2,1)}, u32[]{:S(2)}, u32[]{:S(2)}) collective-permute-start(bf16[768,512]{1,0:T(8,128)(2,1)} %slice_select_fusion.kept), channel_id=1, source_target_pairs={{0,16},{2,18},{1,17},{3,19}} | collective-permute-start | bytes 2359304 | tf_op jit(solution)/shard_map/ppermute | solution.py:499
  6.6 3.6 %collective-permute-start.3 = (bf16[1536,512]{1,0:T(8,128)(2,1)}, bf16[1536,512]{1,0:T(8,128)(2,1)}, u32[]{:S(2)}, u32[]{:S(2)}) collective-permute-start(bf16[1536,512]{1,0:T(8,128)(2,1)} %refs_10_.5), channel_id=1, source_target_pairs={{0,2},{2,4},{4,6},{6,8},{8,10},{10,12},{12,14},{14,16},{16,18},{18... | collective-permute-start | bytes 4718600 | tf_op jit(solution)/shard_map/ppermute | solution.py:479
  13.1 6.6 %shard_map.64 = (bf16[1536,256]{1,0:T(8,128)(2,1)S(1)}, f32[1536,256]{1,0:T(8,128)S(1)}, f32[1536,128]{1,0:T(8,128)S(1)}, f32[8,128]{1,0:T(8,128)S(1)}) custom-call(s32[7]{0:T(128)S(1)} %concatenate.3.refs_0_.info, bf16[1536,512]{1,0:T(8,128)(2,1)S(1)} %copy-done.3, bf16[1536,512]{1,0:T(8,128)(2,1)S(1)} %copy-done, bf16[1536,512]{1,0:T(8,128)(2,1)S(1)} %copy-done.1), custom_call_target="tpu_custom_call" | custom-call | flops 1000 | bytes 1000 | tf_op jit(solution)/shard_map/pallas_call | solution.py:341
  22.6 2.1 %shard_map.65.refs_4_.kept = bf16[768,512]{1,0:T(8,128)(2,1)} custom-call(s32[1]{0:T(128)} %bitcast.3.flag, bf16[768,512]{1,0:T(8,128)(2,1)} %collective-permute-done.1.taken, bf16[768,512]{1,0:T(8,128)(2,1)} %slice_select_fusion.kept, f32[8,128]{1,0:T(8,128)S(1)} %get-tuple-element.25.refs_0_), custom_call_target="tpu_custom_call" | custom-call | flops 1000 | bytes 1000 | tf_op jit(solution)/shard_map/pallas_call | solution.py:369
  24.8 1.6 %collective-permute-start.4 = (bf16[768,512]{1,0:T(8,128)(2,1)}, bf16[768,512]{1,0:T(8,128)(2,1)}, u32[]{:S(2)}, u32[]{:S(2)}) collective-permute-start(bf16[768,512]{1,0:T(8,128)(2,1)} %shard_map.65.refs_4_.kept), channel_id=1, source_target_pairs={{0,8},{16,24},{2,10},{18,26},{1,9},{17,25},{3,11},{19,27}} | collective-permute-start | bytes 2359304 | tf_op jit(solution)/shard_map/ppermute | solution.py:499
  27.8 6.5 %shard_map.66 = (bf16[1536,256]{1,0:T(8,128)(2,1)S(1)}, f32[1536,256]{1,0:T(8,128)S(1)}, f32[1536,128]{1,0:T(8,128)S(1)}, f32[8,128]{1,0:T(8,128)S(1)}) custom-call(s32[7]{0:T(128)S(1)} %concatenate.3.refs_0_.info, bf16[1536,512]{1,0:T(8,128)(2,1)S(1)} %copy-done.4, bf16[1536,512]{1,0:T(8,128)(2,1)S(1)} %copy-done, bf16[1536,512]{1,0:T(8,128)(2,1)S(1)} %copy-done.2, ...), custom_call_target="tpu_custom_call" | custom-call | flops 1000 | bytes 1000 | tf_op jit(solution)/shard_map/pallas_call | solution.py:341
  34.4 3.2 %collective-permute-start.11 = (bf16[1536,256]{1,0:T(8,128)(2,1)S(1)}, bf16[1536,256]{1,0:T(8,128)(2,1)S(1)}, u32[]{:S(2)}, u32[]{:S(2)}) collective-permute-start(bf16[1536,256]{1,0:T(8,128)(2,1)S(1)} %shard_map.67.refs_0_), channel_id=1, source_target_pairs={{0,4},{4,8},{8,12},{12,16},{16,20},{20,24},{24,28},{1,5},{5,9},{9,... | collective-permute-start | bytes 2359304 | tf_op jit(solution)/shard_map/ppermute | solution.py:525
  37.6 2.2 %collective-permute-done.3.values.refs_6_.refs_12_ = bf16[1536,512]{1,0:T(8,128)(2,1)} collective-permute-done((bf16[1536,512]{1,0:T(8,128)(2,1)}, bf16[1536,512]{1,0:T(8,128)(2,1)}, u32[]{:S(2)}, u32[]{:S(2)}) %collective-permute-start.3) | collective-permute-done | bytes 1572896 | tf_op jit(solution)/shard_map/ppermute | solution.py:479
  39.8 1.5 %shard_map.68.refs_1_ = bf16[1536,512]{1,0:T(8,128)(2,1)S(1)} custom-call(bf16[1536,512]{1,0:T(8,128)(2,1)} %collective-permute-done.2.keys.refs_5_.refs_11_, bf16[1536,512]{1,0:T(8,128)(2,1)} %collective-permute-done.3.values.refs_6_.refs_12_, bf16[1536,256]{1,0:T(8,128)(2,1)S(1)} %shard_map.67.refs_0_), custom_call_target="tpu_custom_call" | custom-call | flops 1000 | bytes 1000 | tf_op jit(solution)/shard_map/pallas_call | solution.py:397
  44.0 1.6 %collective-permute-start.5 = (bf16[768,512]{1,0:T(8,128)(2,1)S(1)}, bf16[768,512]{1,0:T(8,128)(2,1)S(1)}, u32[]{:S(2)}, u32[]{:S(2)}) collective-permute-start(bf16[768,512]{1,0:T(8,128)(2,1)S(1)} %shard_map.69.refs_7_.kept), channel_id=1, source_target_pairs={{0,4},{8,12},{16,20},{24,28},{2,6},{10,14},{18,22},{26,30},{1,5},{... | collective-permute-start | bytes 2359304 | tf_op jit(solution)/shard_map/ppermute | solution.py:517
  45.7 7.9 %shard_map.70 = (f32[1536,256]{1,0:T(8,128)S(1)}, f32[1536,128]{1,0:T(8,128)S(1)}, f32[8,128]{1,0:T(8,128)S(1)}) custom-call(s32[7]{0:T(128)S(1)} %concatenate.3.refs_0_.info, bf16[1536,512]{1,0:T(8,128)(2,1)S(1)} %copy-done.5, bf16[1536,256]{1,0:T(8,128)(2,1)S(1)} %copy-done.8, f32[1536,256]{1,0:T(8,128)S(1)} %copy-done.10, f32[1536,128]{1,0:T(8,128)S(1)} %copy-done.12, ...), custom_call_target="tpu_custom_call" | custom-call | flops 8000000000 | bytes 1000 | tf_op jit(solution)/shard_map/pallas_call | solution.py:341
  53.6 7.8 %shard_map.71 = (f32[1536,256]{1,0:T(8,128)S(1)}, f32[1536,128]{1,0:T(8,128)S(1)}, f32[8,128]{1,0:T(8,128)S(1)}) custom-call(s32[7]{0:T(128)S(1)} %concatenate.3.refs_0_.info, bf16[1536,512]{1,0:T(8,128)(2,1)S(1)} %copy-done.5, bf16[1536,256]{1,0:T(8,128)(2,1)S(1)} %get-tuple-element.26.refs_2_, f32[1536,256]{1,0:T(8,128)S(1)} %get-tuple-element.27.refs_3_, ...), custom_call_target="tpu_custom_call" | custom-call | flops 8000000000 | bytes 1000 | tf_op jit(solution)/shard_map/pallas_call | solution.py:341
  61.5 9.1 %collective-permute-done.5.taken = bf16[768,512]{1,0:T(8,128)(2,1)S(1)} collective-permute-done((bf16[768,512]{1,0:T(8,128)(2,1)S(1)}, bf16[768,512]{1,0:T(8,128)(2,1)S(1)}, u32[]{:S(2)}, u32[]{:S(2)}) %collective-permute-start.5) | collective-permute-done | bytes 786464 | tf_op jit(solution)/shard_map/ppermute | solution.py:517
  70.7 3.3 %collective-permute-start.7 = (bf16[1536,256]{1,0:T(8,128)(2,1)S(1)}, bf16[1536,256]{1,0:T(8,128)(2,1)S(1)}, u32[]{:S(2)}, u32[]{:S(2)}) collective-permute-start(bf16[1536,256]{1,0:T(8,128)(2,1)S(1)} %shard_map.72.refs_1_), channel_id=1, source_target_pairs={{0,4},{4,8},{8,12},{12,16},{16,20},{20,24},{24,28},{1,5},{5,9},{9,... | collective-permute-start | bytes 2359304 | tf_op jit(solution)/shard_map/ppermute | solution.py:525
  74.1 7.2 %shard_map.76 = (bf16[768,256]{1,0:T(8,128)(2,1)S(1)}, bf16[768,256]{1,0:T(8,128)(2,1)S(1)}) custom-call(s32[7]{0:T(128)S(1)} %concatenate.3.refs_0_.info, bf16[1536,512]{1,0:T(8,128)(2,1)S(1)} %copy-done.5, bf16[1536,256]{1,0:T(8,128)(2,1)S(1)} %copy-done.8, f32[1536,256]{1,0:T(8,128)S(1)} %get-tuple-element.39.refs_3_, ...), custom_call_target="tpu_custom_call" | custom-call | flops 1000 | bytes 1000 | tf_op jit(solution)/shard_map/pallas_call | solution.py:341
  81.3 1.6 %collective-permute-start.12 = (bf16[768,256]{1,0:T(8,128)(2,1)S(1)}, bf16[768,256]{1,0:T(8,128)(2,1)S(1)}, u32[]{:S(2)}, u32[]{:S(2)}) collective-permute-start(bf16[768,256]{1,0:T(8,128)(2,1)S(1)} %get-tuple-element.44), channel_id=1, source_target_pairs={{0,1},{1,0},{2,3},{3,2},{4,5},{5,4},{6,7},{7,6},{8,9},{9,8},{10,11... | collective-permute-start | bytes 1179656 | tf_op jit(solution)/shard_map/ppermute | solution.py:554
  82.9 1.8 %collective-permute-done.7.refs_7_ = bf16[1536,256]{1,0:T(8,128)(2,1)S(1)} collective-permute-done((bf16[1536,256]{1,0:T(8,128)(2,1)S(1)}, bf16[1536,256]{1,0:T(8,128)(2,1)S(1)}, u32[]{:S(2)}, u32[]{:S(2)}) %collective-permute-start.7) | collective-permute-done | bytes 786464 | tf_op jit(solution)/shard_map/ppermute | solution.py:525
  84.6 4.3 %shard_map.75 = (bf16[768,128]{1,0:T(8,128)(2,1)S(1)}, bf16[768,128]{1,0:T(8,128)(2,1)S(1)}) custom-call(s32[7]{0:T(128)S(1)} %concatenate.3.refs_0_.info, bf16[1536,512]{1,0:T(8,128)(2,1)S(1)} %copy-done.5, bf16[1536,256]{1,0:T(8,128)(2,1)S(1)} %get-tuple-element.26.refs_2_, f32[1536,256]{1,0:T(8,128)S(1)} %get-tuple-element.34.refs_3_, ...), custom_call_target="tpu_custom_call" | custom-call | flops 1000 | bytes 1000 | tf_op jit(solution)/shard_map/pallas_call | solution.py:341
  88.9 1.6 %collective-permute-start.10 = (bf16[768,128]{1,0:T(8,128)(2,1)S(1)}, bf16[768,128]{1,0:T(8,128)(2,1)S(1)}, u32[]{:S(2)}, u32[]{:S(2)}) collective-permute-start(bf16[768,128]{1,0:T(8,128)(2,1)S(1)} %get-tuple-element.38), channel_id=1, source_target_pairs={{0,1},{1,0},{2,3},{3,2},{4,5},{5,4},{6,7},{7,6},{8,9},{9,8},{10,11... | collective-permute-start | bytes 589832 | tf_op jit(solution)/shard_map/ppermute | solution.py:554
  90.5 4.0 %shard_map.74 = (bf16[768,128]{1,0:T(8,128)(2,1)S(1)}, bf16[768,128]{1,0:T(8,128)(2,1)S(1)}) custom-call(s32[7]{0:T(128)S(1)} %concatenate.3.refs_0_.info, bf16[1536,512]{1,0:T(8,128)(2,1)S(1)} %copy-done.5, bf16[1536,256]{1,0:T(8,128)(2,1)S(1)} %get-tuple-element.26.refs_2_, f32[1536,256]{1,0:T(8,128)S(1)} %get-tuple-element.34.refs_3_, ...), custom_call_target="tpu_custom_call" | custom-call | flops 1000 | bytes 1000 | tf_op jit(solution)/shard_map/pallas_call | solution.py:341
  95.1 4.3 %shard_map.77.refs_3_ = f32[768,1536]{1,0:T(8,128)S(1)} custom-call(s32[7]{0:T(128)S(1)} %concatenate.3.refs_0_.info, bf16[768,256]{1,0:T(8,128)(2,1)S(1)} %get-tuple-element.41.refs_0_, bf16[768,128]{1,0:T(8,128)(2,1)S(1)} %get-tuple-element.42.refs_1_, bf16[768,128]{1,0:T(8,128)(2,1)S(1)} %get-tuple-element.43.refs_2_, ...), custom_call_target="tpu_custom_call" | custom-call | flops 1000 | bytes 1000 | tf_op jit(solution)/shard_map/pallas_call | solution.py:442
  100.2 3.4 %shard_map.78 = bf16[768,1536]{1,0:T(8,128)(2,1)} custom-call(s32[7]{0:T(128)S(1)} %concatenate.3.refs_0_.info, bf16[768,128]{1,0:T(8,128)(2,1)S(1)} %collective-permute-done.9.refs_0_, bf16[768,128]{1,0:T(8,128)(2,1)S(1)} %collective-permute-done.10.refs_1_, bf16[1024,1536]{1,0:T(8,128)(2,1)S(1)} %copy-done.6, f32[768,1536]{1,0:T(8,128)S(1)} %shard_map.77.refs_3_), custom_call_target="tpu_custom_call" | custom-call | flops 1000 | bytes 1000 | tf_op jit(solution)/shard_map/pallas_call | solution.py:442
  (49 shorter events, 12.6 us)
Async XLA Ops:
  0.0 10.2 %copy-start = (bf16[1536,512]{1,0:T(8,128)(2,1)S(1)}, bf16[1536,512]{1,0:T(8,128)(2,1)}, u32[]{:S(2)}) copy-start(bf16[1536,512]{1,0:T(8,128)(2,1)} %refs_9_.5) | copy-start | bytes 4718596
  0.0 10.1 %copy-start.14 = (s32[2]{0:T(128)S(1)}, s32[2]{0:T(128)}, u32[]{:S(2)}) copy-start(s32[2]{0:T(128)} %param.10) | copy-start | bytes 28
  0.0 10.2 %copy-start.13 = (s32[2]{0:T(128)S(1)}, s32[2]{0:T(128)}, u32[]{:S(2)}) copy-start(s32[2]{0:T(128)} %param.9) | copy-start | bytes 28
  0.0 2.8 %collective-permute-start = (bf16[1536,512]{1,0:T(8,128)(2,1)}, bf16[1536,512]{1,0:T(8,128)(2,1)S(1)}, u32[]{:S(2)}, u32[]{:S(2)}) collective-permute-start(bf16[1536,512]{1,0:T(8,128)(2,1)} %refs_10_.5), channel_id=1, source_target_pairs={{0,2},{1,3}} | collective-permute-start | bytes 4718600 | tf_op jit(solution)/shard_map/ppermute | solution.py:480
  0.9 36.7 %collective-permute-start.2 = (bf16[1536,512]{1,0:T(8,128)(2,1)}, bf16[1536,512]{1,0:T(8,128)(2,1)}, u32[]{:S(2)}, u32[]{:S(2)}) collective-permute-start(bf16[1536,512]{1,0:T(8,128)(2,1)} %refs_9_.5), channel_id=1, source_target_pairs={{0,2},{2,4},{4,6},{6,8},{8,10},{10,12},{12,14},{14,16},{16,18},{18... | collective-permute-start | bytes 4718600 | tf_op jit(solution)/shard_map/ppermute | solution.py:478
  5.0 17.6 %collective-permute-start.1 = (bf16[768,512]{1,0:T(8,128)(2,1)}, bf16[768,512]{1,0:T(8,128)(2,1)}, u32[]{:S(2)}, u32[]{:S(2)}) collective-permute-start(bf16[768,512]{1,0:T(8,128)(2,1)} %slice_select_fusion.kept), channel_id=1, source_target_pairs={{0,16},{2,18},{1,17},{3,19}} | collective-permute-start | bytes 2359304 | tf_op jit(solution)/shard_map/ppermute | solution.py:499
  6.6 33.3 %collective-permute-start.3 = (bf16[1536,512]{1,0:T(8,128)(2,1)}, bf16[1536,512]{1,0:T(8,128)(2,1)}, u32[]{:S(2)}, u32[]{:S(2)}) collective-permute-start(bf16[1536,512]{1,0:T(8,128)(2,1)} %refs_10_.5), channel_id=1, source_target_pairs={{0,2},{2,4},{4,6},{6,8},{8,10},{10,12},{12,14},{14,16},{16,18},{18... | collective-permute-start | bytes 4718600 | tf_op jit(solution)/shard_map/ppermute | solution.py:479
  10.2 1.4 %copy-start.1 = (bf16[1536,512]{1,0:T(8,128)(2,1)S(1)}, bf16[1536,512]{1,0:T(8,128)(2,1)}, u32[]{:S(2)}) copy-start(bf16[1536,512]{1,0:T(8,128)(2,1)} %refs_10_.5) | copy-start | bytes 4718596
  22.6 3.7 %copy-start.2 = (bf16[1536,512]{1,0:T(8,128)(2,1)S(1)}, bf16[1536,512]{1,0:T(8,128)(2,1)}, u32[]{:S(2)}) copy-start(bf16[1536,512]{1,0:T(8,128)(2,1)} %refs_10_.5) | copy-start | bytes 4718596
  24.8 17.9 %collective-permute-start.4 = (bf16[768,512]{1,0:T(8,128)(2,1)}, bf16[768,512]{1,0:T(8,128)(2,1)}, u32[]{:S(2)}, u32[]{:S(2)}) collective-permute-start(bf16[768,512]{1,0:T(8,128)(2,1)} %shard_map.65.refs_4_.kept), channel_id=1, source_target_pairs={{0,8},{16,24},{2,10},{18,26},{1,9},{17,25},{3,11},{19,27}} | collective-permute-start | bytes 2359304 | tf_op jit(solution)/shard_map/ppermute | solution.py:499
  26.4 1.4 %copy-start.4 = (bf16[1536,512]{1,0:T(8,128)(2,1)S(1)}, bf16[1536,512]{1,0:T(8,128)(2,1)}, u32[]{:S(2)}) copy-start(bf16[1536,512]{1,0:T(8,128)(2,1)} %refs_1_.13) | copy-start | bytes 4718596
  34.4 39.6 %collective-permute-start.11 = (bf16[1536,256]{1,0:T(8,128)(2,1)S(1)}, bf16[1536,256]{1,0:T(8,128)(2,1)S(1)}, u32[]{:S(2)}, u32[]{:S(2)}) collective-permute-start(bf16[1536,256]{1,0:T(8,128)(2,1)S(1)} %shard_map.67.refs_0_), channel_id=1, source_target_pairs={{0,4},{4,8},{8,12},{12,16},{16,20},{20,24},{24,28},{1,5},{5,9},{9,... | collective-permute-start | bytes 2359304 | tf_op jit(solution)/shard_map/ppermute | solution.py:525
  39.8 5.8 %copy-start.12 = (f32[1536,128]{1,0:T(8,128)S(1)}, f32[1536,128]{1,0:T(8,128)}, u32[]{:S(2)}) copy-start(f32[1536,128]{1,0:T(8,128)} %copy-done.11) | copy-start | bytes 2359300
  41.3 32.8 %collective-permute-start.8 = (bf16[1536,512]{1,0:T(8,128)(2,1)S(1)}, bf16[1536,512]{1,0:T(8,128)(2,1)S(1)}, u32[]{:S(2)}, u32[]{:S(2)}) collective-permute-start(bf16[1536,512]{1,0:T(8,128)(2,1)S(1)} %shard_map.68.refs_1_), channel_id=1, source_target_pairs={{0,2},{4,6},{8,10},{12,14},{16,18},{20,22},{24,26},{28,30},{1,3},{... | collective-permute-start | bytes 4718600 | tf_op jit(solution)/shard_map/ppermute | solution.py:515
  42.7 3.0 %copy-start.5 = (bf16[1536,512]{1,0:T(8,128)(2,1)S(1)}, bf16[1536,512]{1,0:T(8,128)(2,1)}, u32[]{:S(2)}) copy-start(bf16[1536,512]{1,0:T(8,128)(2,1)} %refs_1_.13) | copy-start | bytes 4718596
  42.7 3.0 %copy-start.8 = (bf16[1536,256]{1,0:T(8,128)(2,1)S(1)}, bf16[1536,256]{1,0:T(8,128)(2,1)}, u32[]{:S(2)}) copy-start(bf16[1536,256]{1,0:T(8,128)(2,1)} %copy-done.7) | copy-start | bytes 2359300
  42.7 3.0 %copy-start.10 = (f32[1536,256]{1,0:T(8,128)S(1)}, f32[1536,256]{1,0:T(8,128)}, u32[]{:S(2)}) copy-start(f32[1536,256]{1,0:T(8,128)} %copy-done.9) | copy-start | bytes 4718596
  44.0 26.5 %collective-permute-start.5 = (bf16[768,512]{1,0:T(8,128)(2,1)S(1)}, bf16[768,512]{1,0:T(8,128)(2,1)S(1)}, u32[]{:S(2)}, u32[]{:S(2)}) collective-permute-start(bf16[768,512]{1,0:T(8,128)(2,1)S(1)} %shard_map.69.refs_7_.kept), channel_id=1, source_target_pairs={{0,4},{8,12},{16,20},{24,28},{2,6},{10,14},{18,22},{26,30},{1,5},{... | collective-permute-start | bytes 2359304 | tf_op jit(solution)/shard_map/ppermute | solution.py:517
  70.6 3.4 %collective-permute-start.6 = (bf16[768,512]{1,0:T(8,128)(2,1)S(1)}, bf16[768,512]{1,0:T(8,128)(2,1)S(1)}, u32[]{:S(2)}, u32[]{:S(2)}) collective-permute-start(bf16[768,512]{1,0:T(8,128)(2,1)S(1)} %shard_map.73.refs_5_), channel_id=1, source_target_pairs={{0,2},{2,0},{4,6},{6,4},{8,10},{10,8},{12,14},{14,12},{16,18},{18,... | collective-permute-start | bytes 2359304 | tf_op jit(solution)/shard_map/ppermute | solution.py:533
  70.7 13.9 %collective-permute-start.7 = (bf16[1536,256]{1,0:T(8,128)(2,1)S(1)}, bf16[1536,256]{1,0:T(8,128)(2,1)S(1)}, u32[]{:S(2)}, u32[]{:S(2)}) collective-permute-start(bf16[1536,256]{1,0:T(8,128)(2,1)S(1)} %shard_map.72.refs_1_), channel_id=1, source_target_pairs={{0,4},{4,8},{8,12},{12,16},{16,20},{20,24},{24,28},{1,5},{5,9},{9,... | collective-permute-start | bytes 2359304 | tf_op jit(solution)/shard_map/ppermute | solution.py:525
  81.3 13.8 %collective-permute-start.12 = (bf16[768,256]{1,0:T(8,128)(2,1)S(1)}, bf16[768,256]{1,0:T(8,128)(2,1)S(1)}, u32[]{:S(2)}, u32[]{:S(2)}) collective-permute-start(bf16[768,256]{1,0:T(8,128)(2,1)S(1)} %get-tuple-element.44), channel_id=1, source_target_pairs={{0,1},{1,0},{2,3},{3,2},{4,5},{5,4},{6,7},{7,6},{8,9},{9,8},{10,11... | collective-permute-start | bytes 1179656 | tf_op jit(solution)/shard_map/ppermute | solution.py:554
  88.9 10.5 %collective-permute-start.10 = (bf16[768,128]{1,0:T(8,128)(2,1)S(1)}, bf16[768,128]{1,0:T(8,128)(2,1)S(1)}, u32[]{:S(2)}, u32[]{:S(2)}) collective-permute-start(bf16[768,128]{1,0:T(8,128)(2,1)S(1)} %get-tuple-element.38), channel_id=1, source_target_pairs={{0,1},{1,0},{2,3},{3,2},{4,5},{5,4},{6,7},{7,6},{8,9},{9,8},{10,11... | collective-permute-start | bytes 589832 | tf_op jit(solution)/shard_map/ppermute | solution.py:554
  90.5 4.6 %copy-start.6 = (bf16[1024,1536]{1,0:T(8,128)(2,1)S(1)}, bf16[1024,1536]{1,0:T(8,128)(2,1)}, u32[]{:S(2)}) copy-start(bf16[1024,1536]{1,0:T(8,128)(2,1)} %refs_2_.5) | copy-start | bytes 9437188
  94.5 5.7 %collective-permute-start.9 = (bf16[768,128]{1,0:T(8,128)(2,1)S(1)}, bf16[768,128]{1,0:T(8,128)(2,1)S(1)}, u32[]{:S(2)}, u32[]{:S(2)}) collective-permute-start(bf16[768,128]{1,0:T(8,128)(2,1)S(1)} %get-tuple-element.37), channel_id=1, source_target_pairs={{0,1},{1,0},{2,3},{3,2},{4,5},{5,4},{6,7},{7,6},{8,9},{9,8},{10,11... | collective-permute-start | bytes 589832 | tf_op jit(solution)/shard_map/ppermute | solution.py:554
  (4 other events, 4.3 us)

commit v3 on v2

--- a/solution.py
+++ b/solution.py
@@ -556,15 +556,15 @@
 
     for g, (_, count) in enumerate(groups):
         last = g == len(groups) - 1
-        finish(g, [(h, 1) for h in range(count)] if last else [(0, count)], fars[g])
+        finish(g, [(0, count)] if last else [(h, 1) for h in range(count)], fars[g])
     if not paired:
         attended = jnp.concatenate([mine for _, mine, _ in sends], axis=1)
         token_rows = lax.all_to_all(attended, "head", split_axis=0, concat_axis=1, tiled=True)
         return dot(token_rows, out_weight).astype(jnp.bfloat16)
     early = [(mine, place, False) for place, mine, _ in sends]
-    early.append((sends[0][2], sends[0][0], True))
-    late = [(received, place, True) for place, _, received in sends[1:]]
-    base = project(info, early, out_weight, dtype=jnp.float32)
+    early += [(received, place, True) for place, _, received in sends[:-1]]
+    late = [(received, place, True) for place, _, received in sends[-1:]]
+    base = project(info, early, out_weight, dtype=jnp.float32, turns=3)
     return project(info, late, out_weight, base, turns=3)
 
 

time: 105 us -> 116 us (1.10)
  the two profiles are of different devices: /device:TPU:18 before, /device:TPU:24 now
where the time goes in v3:
time: 116 us; the launch traced here: 115 us
  Pallas kernels  56.8 us (49%)
  waiting for transfers between devices  27.2 us (23%)
  starting transfers between devices  21.7 us (19%)
  local copies, waits for them, and re-layouts  7.26 us (6%)
  other arithmetic  2.13 us (2%)
    pallas_call x7, Pallas kernels, stage(): pl.pallas_call(run, in_specs=[SMEM_SPEC] + [VMEM_SPEC] * (n - in_any - 1)...  44.2 us
    ppermute x2, waiting for transfers between devices, send_far(): lax.ppermute(own_last, axis, [(i, i + 2) for i in range(0, size - 2, 2)])  8.93 us
    pallas_call x2, Pallas kernels, project(): pl.pallas_call(kernel, grid=(turns,), in_specs=[SMEM_SPEC] + [VMEM_SPEC]...  7.43 us
    unnamed x30, local copies, waits for them, and re-layouts  7.18 us
    ppermute x2, waiting for transfers between devices, local(): moved = lax.ppermute(held, axis, pairs)  6.78 us
    ppermute x1, waiting for transfers between devices, local(): near_v = lax.ppermute(value_states, axis, onward)  6.58 us
    ppermute x2, starting transfers between devices, send_far(): lax.ppermute(own_last, axis, [(i, i + 2) for i in range(0, size - 2, 2)])  5.66 us
    ppermute x3, waiting for transfers between devices, finish(): received = lax.ppermute(results[1], 'head', [(0, 1), (1, 0)])  4.9 us
  transfers between devices with their start and end apart: 13, of which 4 were waited for; matrix products, arithmetic and copies ran while one was open for 2% of the time, Pallas kernels for 47%

profile of v3, /device:TPU:24, one launch (start us, length us, event | category | flops | bytes accessed | tf_op | source)
XLA Modules:
  0.0 115.4 jit_solution(4943325475950087829)
XLA Ops:
  0.9 1.9 %collective-permute-start.2 = (bf16[1536,512]{1,0:T(8,128)(2,1)}, bf16[1536,512]{1,0:T(8,128)(2,1)}, u32[]{:S(2)}, u32[]{:S(2)}) collective-permute-start(bf16[1536,512]{1,0:T(8,128)(2,1)} %refs_9_.5), channel_id=1, source_target_pairs={{0,2},{2,4},{4,6},{6,8},{8,10},{10,12},{12,14},{14,16},{16,18},{18... | collective-permute-start | bytes 4718600 | tf_op jit(solution)/shard_map/ppermute | solution.py:478
  2.9 2.1 %slice_select_fusion.kept = bf16[768,512]{1,0:T(8,128)(2,1)} fusion(bf16[1536,512]{1,0:T(8,128)(2,1)S(1)} %collective-permute-done, bf16[1536,512]{1,0:T(8,128)(2,1)} %refs_9_.5, pred[]{:T(512)S(6)} %eq.49), kind=kLoop, calls=%fused_computation | loop fusion | flops 393216 | bytes 2359297 | tf_op jit(solution)/shard_map/jit(_where)/select_n | solution.py:481
  5.0 1.6 %collective-permute-start.1 = (bf16[768,512]{1,0:T(8,128)(2,1)}, bf16[768,512]{1,0:T(8,128)(2,1)}, u32[]{:S(2)}, u32[]{:S(2)}) collective-permute-start(bf16[768,512]{1,0:T(8,128)(2,1)} %slice_select_fusion.kept), channel_id=1, source_target_pairs={{0,16},{2,18},{1,17},{3,19}} | collective-permute-start | bytes 2359304 | tf_op jit(solution)/shard_map/ppermute | solution.py:499
  6.6 3.5 %collective-permute-start.3 = (bf16[1536,512]{1,0:T(8,128)(2,1)}, bf16[1536,512]{1,0:T(8,128)(2,1)}, u32[]{:S(2)}, u32[]{:S(2)}) collective-permute-start(bf16[1536,512]{1,0:T(8,128)(2,1)} %refs_10_.5), channel_id=1, source_target_pairs={{0,2},{2,4},{4,6},{6,8},{8,10},{10,12},{12,14},{14,16},{16,18},{18... | collective-permute-start | bytes 4718600 | tf_op jit(solution)/shard_map/ppermute | solution.py:479
  10.2 1.4 %copy-done.1 = bf16[1536,512]{1,0:T(8,128)(2,1)S(1)} copy-done((bf16[1536,512]{1,0:T(8,128)(2,1)S(1)}, bf16[1536,512]{1,0:T(8,128)(2,1)}, u32[]{:S(2)}) %copy-start.1) | copy-done | bytes 1572888
  13.0 6.6 %shard_map.64 = (bf16[1536,256]{1,0:T(8,128)(2,1)S(1)}, f32[1536,256]{1,0:T(8,128)S(1)}, f32[1536,128]{1,0:T(8,128)S(1)}, f32[8,128]{1,0:T(8,128)S(1)}) custom-call(s32[7]{0:T(128)S(1)} %concatenate.3.refs_0_.info, bf16[1536,512]{1,0:T(8,128)(2,1)S(1)} %copy-done.3, bf16[1536,512]{1,0:T(8,128)(2,1)S(1)} %copy-done, bf16[1536,512]{1,0:T(8,128)(2,1)S(1)} %copy-done.1), custom_call_target="tpu_custom_call" | custom-call | flops 1000 | bytes 1000 | tf_op jit(solution)/shard_map/pallas_call | solution.py:341
  22.6 2.1 %shard_map.65.refs_4_.kept = bf16[768,512]{1,0:T(8,128)(2,1)} custom-call(s32[1]{0:T(128)} %bitcast.3.flag, bf16[768,512]{1,0:T(8,128)(2,1)} %collective-permute-done.1.taken, bf16[768,512]{1,0:T(8,128)(2,1)} %slice_select_fusion.kept, f32[8,128]{1,0:T(8,128)S(1)} %get-tuple-element.25.refs_0_), custom_call_target="tpu_custom_call" | custom-call | flops 1000 | bytes 1000 | tf_op jit(solution)/shard_map/pallas_call | solution.py:369
  27.5 6.5 %shard_map.66 = (bf16[1536,256]{1,0:T(8,128)(2,1)S(1)}, f32[1536,256]{1,0:T(8,128)S(1)}, f32[1536,128]{1,0:T(8,128)S(1)}, f32[8,128]{1,0:T(8,128)S(1)}) custom-call(s32[7]{0:T(128)S(1)} %concatenate.3.refs_0_.info, bf16[1536,512]{1,0:T(8,128)(2,1)S(1)} %copy-done.4, bf16[1536,512]{1,0:T(8,128)(2,1)S(1)} %copy-done, bf16[1536,512]{1,0:T(8,128)(2,1)S(1)} %copy-done.2, ...), custom_call_target="tpu_custom_call" | custom-call | flops 1000 | bytes 1000 | tf_op jit(solution)/shard_map/pallas_call | solution.py:341
  34.1 6.6 %collective-permute-done.3.values.refs_6_.refs_12_ = bf16[1536,512]{1,0:T(8,128)(2,1)} collective-permute-done((bf16[1536,512]{1,0:T(8,128)(2,1)}, bf16[1536,512]{1,0:T(8,128)(2,1)}, u32[]{:S(2)}, u32[]{:S(2)}) %collective-permute-start.3) | collective-permute-done | bytes 1572896 | tf_op jit(solution)/shard_map/ppermute | solution.py:479
  40.7 1.5 %shard_map.68.refs_1_ = bf16[1536,512]{1,0:T(8,128)(2,1)S(1)} custom-call(bf16[1536,512]{1,0:T(8,128)(2,1)} %collective-permute-done.2.keys.refs_5_.refs_11_, bf16[1536,512]{1,0:T(8,128)(2,1)} %collective-permute-done.3.values.refs_6_.refs_12_, bf16[1536,256]{1,0:T(8,128)(2,1)S(1)} %shard_map.67.refs_0_), custom_call_target="tpu_custom_call" | custom-call | flops 1000 | bytes 1000 | tf_op jit(solution)/shard_map/pallas_call | solution.py:397
  43.6 6.8 %collective-permute-done.4.taken = bf16[768,512]{1,0:T(8,128)(2,1)} collective-permute-done((bf16[768,512]{1,0:T(8,128)(2,1)}, bf16[768,512]{1,0:T(8,128)(2,1)}, u32[]{:S(2)}, u32[]{:S(2)}) %collective-permute-start.4) | collective-permute-done | bytes 786464 | tf_op jit(solution)/shard_map/ppermute | solution.py:499
  51.7 1.7 %collective-permute-start.5 = (bf16[768,512]{1,0:T(8,128)(2,1)S(1)}, bf16[768,512]{1,0:T(8,128)(2,1)S(1)}, u32[]{:S(2)}, u32[]{:S(2)}) collective-permute-start(bf16[768,512]{1,0:T(8,128)(2,1)S(1)} %shard_map.69.refs_7_.kept), channel_id=1, source_target_pairs={{0,4},{8,12},{16,20},{24,28},{2,6},{10,14},{18,22},{26,30},{1,5},{... | collective-permute-start | bytes 2359304 | tf_op jit(solution)/shard_map/ppermute | solution.py:517
  53.4 7.9 %shard_map.70 = (f32[1536,256]{1,0:T(8,128)S(1)}, f32[1536,128]{1,0:T(8,128)S(1)}, f32[8,128]{1,0:T(8,128)S(1)}) custom-call(s32[7]{0:T(128)S(1)} %concatenate.3.refs_0_.info, bf16[1536,512]{1,0:T(8,128)(2,1)S(1)} %copy-done.5, bf16[1536,256]{1,0:T(8,128)(2,1)S(1)} %copy-done.8, f32[1536,256]{1,0:T(8,128)S(1)} %copy-done.10, f32[1536,128]{1,0:T(8,128)S(1)} %copy-done.12, ...), custom_call_target="tpu_custom_call" | custom-call | flops 8000000000 | bytes 1000 | tf_op jit(solution)/shard_map/pallas_call | solution.py:341
  61.2 7.8 %shard_map.71 = (f32[1536,256]{1,0:T(8,128)S(1)}, f32[1536,128]{1,0:T(8,128)S(1)}, f32[8,128]{1,0:T(8,128)S(1)}) custom-call(s32[7]{0:T(128)S(1)} %concatenate.3.refs_0_.info, bf16[1536,512]{1,0:T(8,128)(2,1)S(1)} %copy-done.5, bf16[1536,256]{1,0:T(8,128)(2,1)S(1)} %get-tuple-element.26.refs_2_, f32[1536,256]{1,0:T(8,128)S(1)} %get-tuple-element.27.refs_3_, ...), custom_call_target="tpu_custom_call" | custom-call | flops 8000000000 | bytes 1000 | tf_op jit(solution)/shard_map/pallas_call | solution.py:341
  69.1 1.9 %collective-permute-start.7 = (bf16[1536,256]{1,0:T(8,128)(2,1)S(1)}, bf16[1536,256]{1,0:T(8,128)(2,1)S(1)}, u32[]{:S(2)}, u32[]{:S(2)}) collective-permute-start(bf16[1536,256]{1,0:T(8,128)(2,1)S(1)} %shard_map.72.refs_1_), channel_id=1, source_target_pairs={{0,4},{4,8},{8,12},{12,16},{16,20},{20,24},{24,28},{1,5},{5,9},{9,... | collective-permute-start | bytes 2359304 | tf_op jit(solution)/shard_map/ppermute | solution.py:525
  71.2 3.7 %collective-permute-start.10 = (bf16[1536,256]{1,0:T(8,128)(2,1)S(1)}, bf16[1536,256]{1,0:T(8,128)(2,1)S(1)}, u32[]{:S(2)}, u32[]{:S(2)}) collective-permute-start(bf16[1536,256]{1,0:T(8,128)(2,1)S(1)} %shard_map.67.refs_0_), channel_id=1, source_target_pairs={{0,4},{4,8},{8,12},{12,16},{16,20},{20,24},{24,28},{1,5},{5,9},{9,... | collective-permute-start | bytes 2359304 | tf_op jit(solution)/shard_map/ppermute | solution.py:525
  75.0 8.9 %collective-permute-done.7.refs_7_ = bf16[1536,256]{1,0:T(8,128)(2,1)S(1)} collective-permute-done((bf16[1536,256]{1,0:T(8,128)(2,1)S(1)}, bf16[1536,256]{1,0:T(8,128)(2,1)S(1)}, u32[]{:S(2)}, u32[]{:S(2)}) %collective-permute-start.7) | collective-permute-done | bytes 786464 | tf_op jit(solution)/shard_map/ppermute | solution.py:525
  83.9 7.1 %shard_map.74 = (bf16[768,256]{1,0:T(8,128)(2,1)S(1)}, bf16[768,256]{1,0:T(8,128)(2,1)S(1)}) custom-call(s32[7]{0:T(128)S(1)} %concatenate.3.refs_0_.info, bf16[1536,512]{1,0:T(8,128)(2,1)S(1)} %copy-done.5, bf16[1536,256]{1,0:T(8,128)(2,1)S(1)} %get-tuple-element.26.refs_2_, f32[1536,256]{1,0:T(8,128)S(1)} %get-tuple-element.34.refs_3_, ...), custom_call_target="tpu_custom_call" | custom-call | flops 1000 | bytes 1000 | tf_op jit(solution)/shard_map/pallas_call | solution.py:341
  91.0 1.6 %collective-permute-start.9 = (bf16[768,256]{1,0:T(8,128)(2,1)S(1)}, bf16[768,256]{1,0:T(8,128)(2,1)S(1)}, u32[]{:S(2)}, u32[]{:S(2)}) collective-permute-start(bf16[768,256]{1,0:T(8,128)(2,1)S(1)} %get-tuple-element.37), channel_id=1, source_target_pairs={{0,1},{1,0},{2,3},{3,2},{4,5},{5,4},{6,7},{7,6},{8,9},{9,8},{10,11... | collective-permute-start | bytes 1179656 | tf_op jit(solution)/shard_map/ppermute | solution.py:554
  92.6 4.3 %shard_map.76 = (bf16[768,128]{1,0:T(8,128)(2,1)S(1)}, bf16[768,128]{1,0:T(8,128)(2,1)S(1)}) custom-call(s32[7]{0:T(128)S(1)} %concatenate.3.refs_0_.info, bf16[1536,512]{1,0:T(8,128)(2,1)S(1)} %copy-done.5, bf16[1536,256]{1,0:T(8,128)(2,1)S(1)} %copy-done.8, f32[1536,256]{1,0:T(8,128)S(1)} %get-tuple-element.38.refs_3_, ...), custom_call_target="tpu_custom_call" | custom-call | flops 1000 | bytes 1000 | tf_op jit(solution)/shard_map/pallas_call | solution.py:341
  98.2 4.0 %shard_map.75 = (bf16[768,128]{1,0:T(8,128)(2,1)S(1)}, bf16[768,128]{1,0:T(8,128)(2,1)S(1)}) custom-call(s32[7]{0:T(128)S(1)} %concatenate.3.refs_0_.info, bf16[1536,512]{1,0:T(8,128)(2,1)S(1)} %copy-done.5, bf16[1536,256]{1,0:T(8,128)(2,1)S(1)} %copy-done.8, f32[1536,256]{1,0:T(8,128)S(1)} %get-tuple-element.38.refs_3_, ...), custom_call_target="tpu_custom_call" | custom-call | flops 1000 | bytes 1000 | tf_op jit(solution)/shard_map/pallas_call | solution.py:341
  103.1 4.9 %collective-permute-done.11.refs_3_ = bf16[768,128]{1,0:T(8,128)(2,1)S(1)} collective-permute-done((bf16[768,128]{1,0:T(8,128)(2,1)S(1)}, bf16[768,128]{1,0:T(8,128)(2,1)S(1)}, u32[]{:S(2)}, u32[]{:S(2)}) %collective-permute-start.11) | collective-permute-done | bytes 196640 | tf_op jit(solution)/shard_map/ppermute | solution.py:554
  108.0 4.3 %shard_map.77.refs_2_ = f32[768,1536]{1,0:T(8,128)S(1)} custom-call(s32[7]{0:T(128)S(1)} %concatenate.3.refs_0_.info, bf16[768,128]{1,0:T(8,128)(2,1)S(1)} %get-tuple-element.40.refs_0_, bf16[768,128]{1,0:T(8,128)(2,1)S(1)} %get-tuple-element.41.refs_1_, bf16[768,256]{1,0:T(8,128)(2,1)S(1)} %get-tuple-element.42.refs_2_, ...), custom_call_target="tpu_custom_call" | custom-call | flops 1000 | bytes 1000 | tf_op jit(solution)/shard_map/pallas_call | solution.py:442
  112.3 3.1 %shard_map.78 = bf16[768,1536]{1,0:T(8,128)(2,1)} custom-call(s32[7]{0:T(128)S(1)} %concatenate.3.refs_0_.info, bf16[768,256]{1,0:T(8,128)(2,1)S(1)} %collective-permute-done.9.refs_0_, bf16[1024,1536]{1,0:T(8,128)(2,1)S(1)} %copy-done.6, f32[768,1536]{1,0:T(8,128)S(1)} %shard_map.77.refs_2_), custom_call_target="tpu_custom_call" | custom-call | flops 1000 | bytes 1000 | tf_op jit(solution)/shard_map/pallas_call | solution.py:442
  (49 shorter events, 13.2 us)
Async XLA Ops:
  0.0 10.2 %copy-start = (bf16[1536,512]{1,0:T(8,128)(2,1)S(1)}, bf16[1536,512]{1,0:T(8,128)(2,1)}, u32[]{:S(2)}) copy-start(bf16[1536,512]{1,0:T(8,128)(2,1)} %refs_9_.5) | copy-start | bytes 4718596
  0.0 10.1 %copy-start.14 = (s32[2]{0:T(128)S(1)}, s32[2]{0:T(128)}, u32[]{:S(2)}) copy-start(s32[2]{0:T(128)} %param.10) | copy-start | bytes 28
  0.0 10.1 %copy-start.13 = (s32[2]{0:T(128)S(1)}, s32[2]{0:T(128)}, u32[]{:S(2)}) copy-start(s32[2]{0:T(128)} %param.9) | copy-start | bytes 28
  0.0 2.8 %collective-permute-start = (bf16[1536,512]{1,0:T(8,128)(2,1)}, bf16[1536,512]{1,0:T(8,128)(2,1)S(1)}, u32[]{:S(2)}, u32[]{:S(2)}) collective-permute-start(bf16[1536,512]{1,0:T(8,128)(2,1)} %refs_10_.5), channel_id=1, source_target_pairs={{0,2},{1,3}} | collective-permute-start | bytes 4718600 | tf_op jit(solution)/shard_map/ppermute | solution.py:480
  0.9 33.2 %collective-permute-start.2 = (bf16[1536,512]{1,0:T(8,128)(2,1)}, bf16[1536,512]{1,0:T(8,128)(2,1)}, u32[]{:S(2)}, u32[]{:S(2)}) collective-permute-start(bf16[1536,512]{1,0:T(8,128)(2,1)} %refs_9_.5), channel_id=1, source_target_pairs={{0,2},{2,4},{4,6},{6,8},{8,10},{10,12},{12,14},{14,16},{16,18},{18... | collective-permute-start | bytes 4718600 | tf_op jit(solution)/shard_map/ppermute | solution.py:478
  5.0 17.6 %collective-permute-start.1 = (bf16[768,512]{1,0:T(8,128)(2,1)}, bf16[768,512]{1,0:T(8,128)(2,1)}, u32[]{:S(2)}, u32[]{:S(2)}) collective-permute-start(bf16[768,512]{1,0:T(8,128)(2,1)} %slice_select_fusion.kept), channel_id=1, source_target_pairs={{0,16},{2,18},{1,17},{3,19}} | collective-permute-start | bytes 2359304 | tf_op jit(solution)/shard_map/ppermute | solution.py:499
  6.6 34.2 %collective-permute-start.3 = (bf16[1536,512]{1,0:T(8,128)(2,1)}, bf16[1536,512]{1,0:T(8,128)(2,1)}, u32[]{:S(2)}, u32[]{:S(2)}) collective-permute-start(bf16[1536,512]{1,0:T(8,128)(2,1)} %refs_10_.5), channel_id=1, source_target_pairs={{0,2},{2,4},{4,6},{6,8},{8,10},{10,12},{12,14},{14,16},{16,18},{18... | collective-permute-start | bytes 4718600 | tf_op jit(solution)/shard_map/ppermute | solution.py:479
  10.2 1.4 %copy-start.1 = (bf16[1536,512]{1,0:T(8,128)(2,1)S(1)}, bf16[1536,512]{1,0:T(8,128)(2,1)}, u32[]{:S(2)}) copy-start(bf16[1536,512]{1,0:T(8,128)(2,1)} %refs_10_.5) | copy-start | bytes 4718596
  22.6 3.5 %copy-start.2 = (bf16[1536,512]{1,0:T(8,128)(2,1)S(1)}, bf16[1536,512]{1,0:T(8,128)(2,1)}, u32[]{:S(2)}) copy-start(bf16[1536,512]{1,0:T(8,128)(2,1)} %refs_10_.5) | copy-start | bytes 4718596
  24.7 25.6 %collective-permute-start.4 = (bf16[768,512]{1,0:T(8,128)(2,1)}, bf16[768,512]{1,0:T(8,128)(2,1)}, u32[]{:S(2)}, u32[]{:S(2)}) collective-permute-start(bf16[768,512]{1,0:T(8,128)(2,1)} %shard_map.65.refs_4_.kept), channel_id=1, source_target_pairs={{0,8},{16,24},{2,10},{18,26},{1,9},{17,25},{3,11},{19,27}} | collective-permute-start | bytes 2359304 | tf_op jit(solution)/shard_map/ppermute | solution.py:499
  26.1 1.4 %copy-start.4 = (bf16[1536,512]{1,0:T(8,128)(2,1)S(1)}, bf16[1536,512]{1,0:T(8,128)(2,1)}, u32[]{:S(2)}) copy-start(bf16[1536,512]{1,0:T(8,128)(2,1)} %refs_1_.14) | copy-start | bytes 4718596
  40.7 12.6 %copy-start.12 = (f32[1536,128]{1,0:T(8,128)S(1)}, f32[1536,128]{1,0:T(8,128)}, u32[]{:S(2)}) copy-start(f32[1536,128]{1,0:T(8,128)} %copy-done.11) | copy-start | bytes 2359300
  42.2 41.7 %collective-permute-start.8 = (bf16[1536,512]{1,0:T(8,128)(2,1)S(1)}, bf16[1536,512]{1,0:T(8,128)(2,1)S(1)}, u32[]{:S(2)}, u32[]{:S(2)}) collective-permute-start(bf16[1536,512]{1,0:T(8,128)(2,1)S(1)} %shard_map.68.refs_1_), channel_id=1, source_target_pairs={{0,2},{4,6},{8,10},{12,14},{16,18},{20,22},{24,26},{28,30},{1,3},{... | collective-permute-start | bytes 4718600 | tf_op jit(solution)/shard_map/ppermute | solution.py:515
  50.4 3.0 %copy-start.5 = (bf16[1536,512]{1,0:T(8,128)(2,1)S(1)}, bf16[1536,512]{1,0:T(8,128)(2,1)}, u32[]{:S(2)}) copy-start(bf16[1536,512]{1,0:T(8,128)(2,1)} %refs_1_.14) | copy-start | bytes 4718596
  50.4 3.0 %copy-start.8 = (bf16[1536,256]{1,0:T(8,128)(2,1)S(1)}, bf16[1536,256]{1,0:T(8,128)(2,1)}, u32[]{:S(2)}) copy-start(bf16[1536,256]{1,0:T(8,128)(2,1)} %copy-done.7) | copy-start | bytes 2359300
  50.4 3.0 %copy-start.10 = (f32[1536,256]{1,0:T(8,128)S(1)}, f32[1536,256]{1,0:T(8,128)}, u32[]{:S(2)}) copy-start(f32[1536,256]{1,0:T(8,128)} %copy-done.9) | copy-start | bytes 4718596
  51.7 19.4 %collective-permute-start.5 = (bf16[768,512]{1,0:T(8,128)(2,1)S(1)}, bf16[768,512]{1,0:T(8,128)(2,1)S(1)}, u32[]{:S(2)}, u32[]{:S(2)}) collective-permute-start(bf16[768,512]{1,0:T(8,128)(2,1)S(1)} %shard_map.69.refs_7_.kept), channel_id=1, source_target_pairs={{0,4},{8,12},{16,20},{24,28},{2,6},{10,14},{18,22},{26,30},{1,5},{... | collective-permute-start | bytes 2359304 | tf_op jit(solution)/shard_map/ppermute | solution.py:517
  69.1 14.8 %collective-permute-start.7 = (bf16[1536,256]{1,0:T(8,128)(2,1)S(1)}, bf16[1536,256]{1,0:T(8,128)(2,1)S(1)}, u32[]{:S(2)}, u32[]{:S(2)}) collective-permute-start(bf16[1536,256]{1,0:T(8,128)(2,1)S(1)} %shard_map.72.refs_1_), channel_id=1, source_target_pairs={{0,4},{4,8},{8,12},{12,16},{16,20},{20,24},{24,28},{1,5},{5,9},{9,... | collective-permute-start | bytes 2359304 | tf_op jit(solution)/shard_map/ppermute | solution.py:525
  71.2 12.8 %collective-permute-start.6 = (bf16[768,512]{1,0:T(8,128)(2,1)S(1)}, bf16[768,512]{1,0:T(8,128)(2,1)S(1)}, u32[]{:S(2)}, u32[]{:S(2)}) collective-permute-start(bf16[768,512]{1,0:T(8,128)(2,1)S(1)} %shard_map.73.refs_5_), channel_id=1, source_target_pairs={{0,2},{2,0},{4,6},{6,4},{8,10},{10,8},{12,14},{14,12},{16,18},{18,... | collective-permute-start | bytes 2359304 | tf_op jit(solution)/shard_map/ppermute | solution.py:533
  71.2 21.4 %collective-permute-start.10 = (bf16[1536,256]{1,0:T(8,128)(2,1)S(1)}, bf16[1536,256]{1,0:T(8,128)(2,1)S(1)}, u32[]{:S(2)}, u32[]{:S(2)}) collective-permute-start(bf16[1536,256]{1,0:T(8,128)(2,1)S(1)} %shard_map.67.refs_0_), channel_id=1, source_target_pairs={{0,4},{4,8},{8,12},{12,16},{16,20},{20,24},{24,28},{1,5},{5,9},{9,... | collective-permute-start | bytes 2359304 | tf_op jit(solution)/shard_map/ppermute | solution.py:525
  91.0 21.3 %collective-permute-start.9 = (bf16[768,256]{1,0:T(8,128)(2,1)S(1)}, bf16[768,256]{1,0:T(8,128)(2,1)S(1)}, u32[]{:S(2)}, u32[]{:S(2)}) collective-permute-start(bf16[768,256]{1,0:T(8,128)(2,1)S(1)} %get-tuple-element.37), channel_id=1, source_target_pairs={{0,1},{1,0},{2,3},{3,2},{4,5},{5,4},{6,7},{7,6},{8,9},{9,8},{10,11... | collective-permute-start | bytes 1179656 | tf_op jit(solution)/shard_map/ppermute | solution.py:554
  96.9 6.2 %collective-permute-start.12 = (bf16[768,128]{1,0:T(8,128)(2,1)S(1)}, bf16[768,128]{1,0:T(8,128)(2,1)S(1)}, u32[]{:S(2)}, u32[]{:S(2)}) collective-permute-start(bf16[768,128]{1,0:T(8,128)(2,1)S(1)} %get-tuple-element.44), channel_id=1, source_target_pairs={{0,1},{1,0},{2,3},{3,2},{4,5},{5,4},{6,7},{7,6},{8,9},{9,8},{10,11... | collective-permute-start | bytes 589832 | tf_op jit(solution)/shard_map/ppermute | solution.py:554
  98.2 9.8 %copy-start.6 = (bf16[1024,1536]{1,0:T(8,128)(2,1)S(1)}, bf16[1024,1536]{1,0:T(8,128)(2,1)}, u32[]{:S(2)}) copy-start(bf16[1024,1536]{1,0:T(8,128)(2,1)} %refs_1_.15) | copy-start | bytes 9437188
  102.2 5.7 %collective-permute-start.11 = (bf16[768,128]{1,0:T(8,128)(2,1)S(1)}, bf16[768,128]{1,0:T(8,128)(2,1)S(1)}, u32[]{:S(2)}, u32[]{:S(2)}) collective-permute-start(bf16[768,128]{1,0:T(8,128)(2,1)S(1)} %get-tuple-element.43), channel_id=1, source_target_pairs={{0,1},{1,0},{2,3},{3,2},{4,5},{5,4},{6,7},{7,6},{8,9},{9,8},{10,11... | collective-permute-start | bytes 589832 | tf_op jit(solution)/shard_map/ppermute | solution.py:554
  (4 other events, 4.3 us)
